TPU v7x, 32 devices: a whole 2x2x4 slice. The times are simulated.
32 devices in a mesh: groups: 2 (over x), gx: 16 (over z, y, core).
Axes of the slice: x: 2, y: 2, z: 4, core: 2. Of those that a mesh axis runs over, the one named last changes fastest.
Arguments:
- lifted_field: bfloat16 [20, 128, 128, 512], P(None, ('groups', 'gx')), parts along dimension 1, may hold values from -6 to 6
- saturation_grad: bfloat16 [128, 128, 512], P(('groups', 'gx')), parts along dimension 0, may hold values from -6 to 6
- readout: float32 [20], replicated, may hold values from -3 to 3
- spectral_weight: bfloat16 [2, 20, 20, 24, 1152], P(None, None, None, None, 'gx'), may hold values from -3 to 3
- point_weight: bfloat16 [20, 20], replicated, may hold values from -1.25 to 1.25
- point_bias: float32 [20], replicated, may hold values from -3 to 3
Outputs:
- grad_field: bfloat16 [20, 128, 128, 512], P(None, ('groups', 'gx')), parts along dimension 1
- grad_spectral: float32 [4, 20, 20, 24, 1152], P('groups', None, None, None, 'gx'), parts along dimension 0
- grad_point: float32 [40, 20], P('groups'), parts along dimension 0
- grad_bias: float32 [40], P('groups'), parts along dimension 0
There are 2 independent parts, one for each index of `groups`. A program takes and returns all parts, laid end to end along the dimension named above; an argument that names none is the same for every part. Nothing has to cross between parts.
All inputs are finite; a program needn't handle non-finite values.
Results may differ from a plain program's by a relative error of at most 0.02.
Values may be sent and summed in bfloat16 or wider, within the bound.
A program may use at most 256 MiB of HBM per device.

v0:
```python
from functools import partial
import math

import jax
import jax.numpy as jnp
import numpy as np
from jax import lax
from jax.experimental import pallas as pl
from jax.experimental.pallas import tpu as pltpu
from jax.sharding import PartitionSpec as P

NY = 128
NZ = 32
NT = 16
MX = 12
MY = 12
MZ = 6
MT = 4
NZT = 512
KZT = 48
KY = 2 * MY
KX = 2 * MX
LANES = 128
YB = 32
BF = jnp.bfloat16
F32 = jnp.float32
MESH = pl.DeviceIdType.MESH


def axis_tables(length, kept):
    positions = np.arange(length)
    frequency = np.concatenate([np.arange(kept), np.arange(length - kept, length)])
    angles = (frequency[:, None] * positions[None, :] % length) * (2.0 * math.pi / length)
    factor = 1.0 / math.sqrt(length)
    return np.cos(angles) * factor, np.sin(angles) * factor


def plane_tables():
    depth = np.concatenate([np.arange(MZ), np.arange(NZ - MZ, NZ)])
    phases = (
        depth[None, None, :, None] * np.arange(NZ)[:, None, None, None] * NT
        + np.arange(MT)[None, None, None, :] * np.arange(NT)[None, :, None, None] * NZ
    ) % NZT
    angles = phases * (2.0 * math.pi / NZT)
    factor = 1.0 / math.sqrt(NZT)
    cos_part = (np.cos(angles) * factor).reshape(NZT, KZT)
    sin_part = (np.sin(angles) * factor).reshape(NZT, KZT)
    weights = np.tile(np.where(np.arange(MT) == 0, 1.0, 2.0), 2 * MZ)
    forward = np.zeros((NZT, 2 * LANES))
    forward[:, :KZT], forward[:, LANES : LANES + KZT] = cos_part, -sin_part
    inverse = np.zeros((NZT, 2 * LANES))
    inverse[:, :KZT], inverse[:, LANES : LANES + KZT] = cos_part * weights, -sin_part * weights
    return forward, inverse


def narrow(table):
    return jnp.asarray(np.asarray(table, np.float32).astype(jnp.bfloat16))


def lateral_tables(rows):
    c, s = axis_tables(NY, MY)
    same = np.eye(rows)
    pairs = np.array([[c, s], [-s, c]])
    forward = np.einsum("rqky,xw->krxqwy", pairs, same)
    forward = forward.reshape(KY * 2 * rows, 2, rows, NY // YB, YB)
    forward = forward.transpose(3, 0, 1, 2, 4).reshape(NY // YB, KY * 2 * rows, 2 * rows * YB)
    inverse = np.einsum("rqky,xw->qwykrx", pairs, same)
    inverse = inverse.reshape(2, rows, NY // YB, YB, KY * 2 * rows)
    inverse = inverse.transpose(2, 0, 1, 3, 4).reshape(NY // YB, 2 * rows * YB, KY * 2 * rows)
    whole = np.einsum("rqky,xw->krxqwy", pairs, same).reshape(KY * 2 * rows, 2 * rows * NY)
    return narrow(forward), narrow(inverse), narrow(whole)


def stream_tables(cells, rows):
    c, s = axis_tables(cells, MX)
    pairs = np.array([[c, s], [-s, c]]).reshape(2, 2, KX, cells // rows, rows)
    table = np.einsum("rqkdx,ab->arkdbqx", pairs, np.eye(2))
    table = table.reshape(4 * KX, cells * 4)
    return narrow(table), narrow(table.T)


def mode_pieces(n):
    per = KY * KZT // n
    out = []
    for d in range(n):
        at, end, pieces = d * per, (d + 1) * per, []
        while at < end:
            ky, col = divmod(at, KZT)
            width = min(KZT - col, end - at)
            pieces.append((ky, col, width))
            at += width
        out.append(pieces)
    return out


def params(mib, **more):
    return pltpu.CompilerParams(vmem_limit_bytes=mib << 20, **more)


def dot(a, b):
    return jnp.dot(a, b, preferred_element_type=F32)


def pack(spectrum, out_ref, first_row, n, rr):
    for d, pieces in enumerate(mode_pieces(n)):
        halves = []
        for half in range(2):
            at = half * LANES
            parts = [
                spectrum[ky * rr : (ky + 1) * rr, at + col : at + col + width]
                for ky, col, width in pieces
            ]
            halves.append(jnp.concatenate(parts, axis=1))
        out_ref[d, pl.ds(first_row, 2 * rr), :] = jnp.concatenate(halves, axis=0).astype(BF)


def forward_kernel(n, rr, field_ref, plane_ref, lateral_ref, out_ref):
    cells = field_ref.shape[1] * NY
    flats = [
        dot(field_ref[half].reshape(cells, NZT), plane_ref[...]).astype(BF) for half in range(2)
    ]
    real = jnp.concatenate([f[:, :LANES] for f in flats], axis=1)
    imag = jnp.concatenate([f[:, LANES:] for f in flats], axis=1)
    spectrum = dot(lateral_ref[...], jnp.concatenate([real, imag], axis=0))
    pack(spectrum, out_ref, 0, n, rr)


def forward_call(field, plane_table, lateral_whole, n):
    channels, rows = field.shape[:2]
    rr = 2 * rows
    per = KY * KZT // n
    return pl.pallas_call(
        partial(forward_kernel, n, rr),
        grid=(channels // 2,),
        out_shape=jax.ShapeDtypeStruct((n, channels * rr, per), BF),
        in_specs=[
            pl.BlockSpec((2, rows, NY, NZT), lambda c: (c, 0, 0, 0)),
            pl.BlockSpec(plane_table.shape, lambda c: (0, 0)),
            pl.BlockSpec(lateral_whole.shape, lambda c: (0, 0)),
        ],
        out_specs=pl.BlockSpec((n, 2 * rr, per), lambda c: (0, c, 0)),
        compiler_params=params(40),
        name="forward",
    )(field, plane_table, lateral_whole)


def exchange(n, source, target, send, recv, local):
    me, group = lax.axis_index("gx"), lax.axis_index("groups")
    copies = []
    for k in range(1, n):
        peer = lax.rem(me + k, n)
        copy = pltpu.make_async_remote_copy(
            src_ref=source.at[peer],
            dst_ref=target.at[me],
            send_sem=send.at[k],
            recv_sem=recv.at[k],
            device_id=(group, peer),
            device_id_type=MESH,
        )
        copy.start()
        copies.append(copy)
    own = pltpu.make_async_copy(source.at[me], target.at[me], local)
    own.start()
    own.wait()
    return copies


def mix_kernel(
    n, rr, adjoint, sent, weight_hbm, stream_ref, back_ref, rows_out, spec_out,
    got, weights, mixed_wire, got_back, send, recv, local, weight_sem,
):
    channels = spec_out.shape[0]
    per = spec_out.shape[2]
    me, group = lax.axis_index("gx"), lax.axis_index("groups")
    barrier = pltpu.get_barrier_semaphore()
    for k in range(1, n):
        pl.semaphore_signal(
            barrier, inc=1, device_id=(group, lax.rem(me + k, n)), device_id_type=MESH
        )
    fetch = pltpu.make_async_copy(weight_hbm, weights, weight_sem)
    fetch.start()
    pl.semaphore_wait(barrier, n - 1)
    copies = exchange(n, sent, got, send.at[0], recv.at[0], local.at[0])
    for copy in copies:
        copy.wait()

    @pl.loop(0, channels // 2)
    def _(pair):
        block = got[:, pl.ds(pl.multiple_of(pair * 2 * rr, 16), 2 * rr), :]
        both = dot(stream_ref[...], block.reshape(n * 2 * rr, per))
        spec_out[2 * pair] = both[: 2 * KX]
        spec_out[2 * pair + 1] = both[2 * KX :]

    fetch.wait()

    @pl.loop(0, channels // 2)
    def _(pair):
        results = []
        for half in range(2):
            o = 2 * pair + half
            real = jnp.zeros((KX, per), F32)
            imag = jnp.zeros((KX, per), F32)
            for i in range(channels):
                at = (o, i) if adjoint else (i, o)
                w_real = weights[0, at[0], at[1]].astype(F32)
                w_imag = weights[1, at[0], at[1]].astype(F32)
                s_real = spec_out[i, :KX]
                s_imag = spec_out[i, KX:]
                if adjoint:
                    real += w_real * s_real + w_imag * s_imag
                    imag += w_real * s_imag - w_imag * s_real
                else:
                    real += w_real * s_real - w_imag * s_imag
                    imag += w_real * s_imag + w_imag * s_real
            results += [real, imag]
        both = dot(back_ref[...], jnp.concatenate(results, axis=0).astype(BF)).astype(BF)
        mixed_wire[:, pl.ds(pl.multiple_of(pair * 2 * rr, 16), 2 * rr), :] = both.reshape(
            n, 2 * rr, per
        )

    copies = exchange(n, mixed_wire, got_back, send.at[1], recv.at[1], local.at[1])
    for copy in copies:
        copy.wait()

    pieces_of = mode_pieces(n)

    @pl.loop(0, channels // 2)
    def _(pair):
        found = [[[] for _ in range(KY)] for _ in range(2)]
        for d in range(n):
            block = got_back[d, pl.ds(pl.multiple_of(pair * 2 * rr, 16), 2 * rr), :].astype(F32)
            at = 0
            for ky, _, width in pieces_of[d]:
                for half in range(2):
                    found[half][ky].append(block[half * rr : (half + 1) * rr, at : at + width])
                at += width
        lanes = jnp.zeros((rr, LANES - KZT), F32)
        halves = [
            jnp.concatenate(
                [jnp.concatenate(found[half][ky] + [lanes], axis=1) for ky in range(KY)], axis=0
            )
            for half in range(2)
        ]
        rows_out[pair] = jnp.concatenate(halves, axis=1).astype(BF)


def mix_call(sent, weight, stream, stream_back, n, adjoint):
    channels = weight.shape[1]
    rr = sent.shape[1] // channels
    per = sent.shape[2]
    return pl.pallas_call(
        partial(mix_kernel, n, rr, adjoint),
        out_shape=(
            jax.ShapeDtypeStruct((channels // 2, KY * rr, 2 * LANES), BF),
            jax.ShapeDtypeStruct((channels, 2 * KX, per), F32),
        ),
        in_specs=[
            pl.BlockSpec(memory_space=pltpu.VMEM),
            pl.BlockSpec(memory_space=pl.ANY),
            pl.BlockSpec(memory_space=pltpu.VMEM),
            pl.BlockSpec(memory_space=pltpu.VMEM),
        ],
        out_specs=(
            pl.BlockSpec(memory_space=pltpu.VMEM),
            pl.BlockSpec(memory_space=pltpu.VMEM),
        ),
        scratch_shapes=[
            pltpu.VMEM(sent.shape, BF),
            pltpu.VMEM(weight.shape, BF),
            pltpu.VMEM(sent.shape, BF),
            pltpu.VMEM(sent.shape, BF),
            pltpu.SemaphoreType.DMA((2, n)),
            pltpu.SemaphoreType.DMA((2, n)),
            pltpu.SemaphoreType.DMA((2,)),
            pltpu.SemaphoreType.DMA(()),
        ],
        compiler_params=params(40, collective_id=int(adjoint), has_side_effects=True),
        name="adjoint_mix" if adjoint else "mix",
    )(sent, weight, stream, stream_back)


def gelu_slope(v):
    a = jnp.abs(v)
    t = 1.0 / (1.0 + (0.3275911 * 0.7071067811865476) * a)
    e = jnp.exp(-0.5 * v * v)
    poly = 0.5 * 1.061405429
    for coefficient in (-1.453152027, 1.421413741, -0.284496736, 0.254829592):
        poly = poly * t + 0.5 * coefficient
    tail = e * (poly * t - 0.3989422804014327 * a)
    return jnp.where(v >= 0, 1.0 - tail, tail)


def planes(rows_ref, lateral, table, store, channels, cells):
    @pl.loop(0, channels // 2)
    def _(pair):
        flat = dot(lateral, rows_ref[pair]).astype(BF)
        for half in range(2):
            at = slice(half * LANES, (half + 1) * LANES)
            plane = jnp.concatenate([flat[:cells, at], flat[cells:, at]], axis=1)
            store(2 * pair + half, dot(plane, table))


def middle_kernel(
    n, rr, rows_ref, field_ref, sat_ref, readout_ref, bias_ref, kron_ref, inverse_ref, back_ref,
    lat_inv_ref, lat_fwd_ref, grad_ref, wire_ref, corr_ref, spectral, spectrum,
):
    step = pl.program_id(0)
    channels, rows = field_ref.shape[:2]
    cells = rows * YB

    @pl.when(step == 0)
    def _():
        corr_ref[...] = jnp.zeros_like(corr_ref)
        spectrum[...] = jnp.zeros_like(spectrum)

    def keep(o, value):
        spectral[o] = value.reshape(rows, YB, NZT)

    planes(rows_ref, lat_inv_ref[0], inverse_ref[...], keep, channels, cells)

    @pl.loop(0, rows)
    def _(x):
        @pl.loop(0, YB // 8)
        def _(yb):
            y8 = pl.ds(pl.multiple_of(yb * 8, 8), 8)
            block = field_ref[:, x, y8, :].reshape(channels * 8, NZT)
            point = dot(kron_ref[...], block)
            bias = jnp.concatenate([bias_ref[...]] * (NZT // LANES), axis=1)
            readout = jnp.concatenate([readout_ref[...]] * (NZT // LANES), axis=1)
            pre = point + spectral[:, x, y8, :].reshape(channels * 8, NZT) + bias
            sat = sat_ref[x, y8, :].astype(F32)
            up = readout * jnp.broadcast_to(sat[None], (channels, 8, NZT)).reshape(-1, NZT)
            grad = (up * gelu_slope(pre)).astype(BF)
            grad_ref[:, x, y8, :] = grad.reshape(channels, 8, NZT)
            left = jnp.concatenate([block, jnp.ones((16, NZT), BF)], axis=0)
            corr_ref[...] += lax.dot_general(
                left, grad, (((1,), (1,)), ((), ())), preferred_element_type=F32
            )

    @pl.loop(0, channels // 2)
    def _(pair):
        flats = [
            dot(grad_ref[2 * pair + half].reshape(cells, NZT), back_ref[...]).astype(BF)
            for half in range(2)
        ]
        real = jnp.concatenate([f[:, :LANES] for f in flats], axis=1)
        imag = jnp.concatenate([f[:, LANES:] for f in flats], axis=1)
        spectrum[pair] += dot(lat_fwd_ref[0], jnp.concatenate([real, imag], axis=0))

    @pl.when(step == pl.num_programs(0) - 1)
    def _():
        @pl.loop(0, channels // 2)
        def _(pair):
            pack(spectrum[pair], wire_ref, pl.multiple_of(pair * 2 * rr, 16), n, rr)


def middle_call(rows_in, field, sat, readout, bias, kron, inverse, back, lat_inv, lat_fwd, n):
    channels, rows = field.shape[:2]
    rr = 2 * rows
    per = KY * KZT // n
    whole = lambda a: pl.BlockSpec(a.shape, lambda y: (0,) * a.ndim)
    return pl.pallas_call(
        partial(middle_kernel, n, rr),
        grid=(NY // YB,),
        out_shape=(
            jax.ShapeDtypeStruct(field.shape, BF),
            jax.ShapeDtypeStruct((n, channels * rr, per), BF),
            jax.ShapeDtypeStruct((channels * 8 + 16, channels * 8), F32),
        ),
        in_specs=[
            whole(rows_in),
            pl.BlockSpec((channels, rows, YB, NZT), lambda y: (0, 0, y, 0)),
            pl.BlockSpec((rows, YB, NZT), lambda y: (0, y, 0)),
            whole(readout), whole(bias), whole(kron), whole(inverse), whole(back),
            pl.BlockSpec((1,) + lat_inv.shape[1:], lambda y: (y, 0, 0)),
            pl.BlockSpec((1,) + lat_fwd.shape[1:], lambda y: (y, 0, 0)),
        ],
        out_specs=(
            pl.BlockSpec((channels, rows, YB, NZT), lambda y: (0, 0, y, 0)),
            pl.BlockSpec((n, channels * rr, per), lambda y: (0, 0, 0)),
            pl.BlockSpec((channels * 8 + 16, channels * 8), lambda y: (0, 0)),
        ),
        scratch_shapes=[
            pltpu.VMEM((channels, rows, YB, NZT), F32),
            pltpu.VMEM((channels // 2, KY * rr, 2 * LANES), F32),
        ],
        compiler_params=params(48),
        name="middle",
    )(rows_in, field, sat, readout, bias, kron, inverse, back, lat_inv, lat_fwd)


def last_kernel(rows_ref, grad_ref, kron_ref, table_ref, lat_inv_ref, out_ref, spectral):
    channels, rows = grad_ref.shape[:2]
    cells = rows * YB

    def keep(o, value):
        spectral[o] = value.reshape(rows, YB, NZT)

    planes(rows_ref, lat_inv_ref[0], table_ref[...], keep, channels, cells)

    @pl.loop(0, rows)
    def _(x):
        @pl.loop(0, YB // 8)
        def _(yb):
            y8 = pl.ds(pl.multiple_of(yb * 8, 8), 8)
            block = grad_ref[:, x, y8, :].reshape(channels * 8, NZT)
            total = dot(kron_ref[...], block) + spectral[:, x, y8, :].reshape(channels * 8, NZT)
            out_ref[:, x, y8, :] = total.astype(BF).reshape(channels, 8, NZT)


def last_call(rows_in, grad, kron, table, lat_inv):
    channels, rows = grad.shape[:2]
    whole = lambda a: pl.BlockSpec(a.shape, lambda y: (0,) * a.ndim)
    block = pl.BlockSpec((channels, rows, YB, NZT), lambda y: (0, 0, y, 0))
    return pl.pallas_call(
        last_kernel,
        grid=(NY // YB,),
        out_shape=jax.ShapeDtypeStruct(grad.shape, BF),
        in_specs=[
            whole(rows_in), block, whole(kron), whole(table),
            pl.BlockSpec((1,) + lat_inv.shape[1:], lambda y: (y, 0, 0)),
        ],
        out_specs=block,
        scratch_shapes=[pltpu.VMEM((channels, rows, YB, NZT), F32)],
        compiler_params=params(48),
        name="last",
    )(rows_in, grad, kron, table, lat_inv)


def outer_kernel(spec_ref, back_ref, out_ref):
    s_real, s_imag = spec_ref[0, :KX], spec_ref[0, KX:]
    for o in range(back_ref.shape[0]):
        b_real, b_imag = back_ref[o, :KX], back_ref[o, KX:]
        out_ref[0, 0, o] = s_real * b_real + s_imag * b_imag
        out_ref[1, 0, o] = s_real * b_imag - s_imag * b_real


def outer_call(spec, back):
    channels, _, per = spec.shape
    return pl.pallas_call(
        outer_kernel,
        grid=(channels,),
        out_shape=jax.ShapeDtypeStruct((2, channels, channels, KX, per), F32),
        in_specs=[
            pl.BlockSpec((1, 2 * KX, per), lambda i: (i, 0, 0)),
            pl.BlockSpec(back.shape, lambda i: (0, 0, 0)),
        ],
        out_specs=pl.BlockSpec((2, 1, channels, KX, per), lambda i: (0, i, 0, 0, 0)),
        compiler_params=params(24),
        name="outer",
    )(spec, back)


def local(n, lifted_field, saturation_grad, readout, spectral_weight, point_weight, point_bias):
    channels, rows = lifted_field.shape[:2]
    forward_table, inverse_table = plane_tables()
    lat_fwd, lat_inv, lat_whole = lateral_tables(rows)
    stream, stream_back = stream_tables(rows * n, rows)
    eye = jnp.eye(8, dtype=BF)
    kron = jnp.kron(point_weight, eye)
    spread = lambda a: jnp.broadcast_to(jnp.repeat(a, 8)[:, None], (channels * 8, LANES))

    sent = forward_call(lifted_field, narrow(forward_table), lat_whole, n)
    rows_in, spec = mix_call(sent, spectral_weight, stream, stream_back, n, False)
    grad_pre, sent_back, corr = middle_call(
        rows_in, lifted_field, saturation_grad, spread(readout), spread(point_bias), kron.T,
        narrow(inverse_table.T), narrow(inverse_table), lat_inv, lat_fwd, n,
    )
    diagonal = jnp.einsum("iaoa->io", corr[: channels * 8].reshape(channels, 8, channels, 8))
    bias_part = corr[channels * 8].reshape(channels, 8).sum(axis=1)
    grad_point, grad_bias = lax.psum((diagonal, bias_part), "gx")
    rows_back, back_spec = mix_call(sent_back, spectral_weight, stream, stream_back, n, True)
    grad_spectral = outer_call(spec, back_spec)
    grad_field = last_call(rows_back, grad_pre, kron, narrow(forward_table.T), lat_inv)
    return (grad_field, grad_spectral, grad_point, grad_bias)


def solution(mesh):
    placed = (
        P(None, ("groups", "gx"), None, None),
        P(("groups", "gx"), None, None),
        P(),
        P(None, None, None, None, "gx"),
        P(),
        P(),
    )
    return jax.shard_map(
        partial(local, mesh.shape["gx"]),
        mesh=mesh,
        in_specs=placed,
        out_specs=(
            P(None, ("groups", "gx"), None, None),
            P("groups", None, None, None, "gx"),
            P("groups", None),
            P("groups"),
        ),
        check_vma=False,
    )
```

profile of v0, /device:TPU:0, one launch (start us, length us, event | category | flops | bytes accessed | tf_op | source)
XLA Modules:
  0.0 285.3 jit_solution(9982169230496113821)
XLA Ops:
  0.6 4.0 %copy-done = bf16[20,4,128,512]{3,2,1,0:T(8,128)(2,1)S(1)} copy-done((bf16[20,4,128,512]{3,2,1,0:T(8,128)(2,1)S(1)}, bf16[20,4,128,512]{3,2,1,0:T(8,128)(2,1)}, u32[]{:S(2)}) %copy-start) | copy-done | bytes 10485784
  4.6 1.0 copy-done.5
  5.6 0.9 copy-done.9
  6.6 8.9 %forward.1.sent = bf16[16,160,72]{2,1,0:T(8,128)(2,1)S(1)} custom-call(bf16[20,4,128,512]{3,2,1,0:T(8,128)(2,1)S(1)} %copy-done, bf16[512,256]{1,0:T(8,128)(2,1)S(1)} %copy-done.9, bf16[192,1024]{1,0:T(8,128)(2,1)S(1)} %copy-done.5), custom_call_target="tpu_custom_call" | custom-call | tf_op jit(solution)/shard_map/forward/pallas_call | solution.py:132
  15.6 37.0 %mix.1 = (bf16[10,192,256]{2,1,0:T(8,128)(2,1)S(1)}, f32[20,48,72]{2,1,0:T(8,128)S(1)}) custom-call(bf16[16,160,72]{2,1,0:T(8,128)(2,1)S(1)} %forward.1.sent, bf16[2,20,20,24,72]{4,3,2,1,0:T(8,128)(2,1)S(1)} %copy-done.1, bf16[96,256]{1,0:T(8,128)(2,1)S(1)} %copy-done.12, bf16[256,96]{1,0:T(8,128)(2,1)S(1)} %copy-done.8), custom_call_target="tpu_custom_call" | custom-call | tf_op jit(solution)/shard_map/mix/pallas_call | solution.py:251
  52.7 1.1 broadcast_multiply_fusion
  53.7 1.8 mul.27.kron_ref
  55.6 0.1 copy.20
  55.7 0.1 broadcast_in_dim.31
  56.0 0.1 broadcast_in_dim.34
  56.2 1.0 copy-done.6
  57.2 0.9 copy-done.10
  58.2 0.9 copy-done.11
  59.1 78.1 %middle.1 = (bf16[20,4,128,512]{3,2,1,0:T(8,128)(2,1)}, bf16[16,160,72]{2,1,0:T(8,128)(2,1)S(1)}, f32[176,160]{1,0:T(8,128)S(1)}) custom-call(bf16[10,192,256]{2,1,0:T(8,128)(2,1)S(1)} %get-tuple-element.11.rows_ref, bf16[20,4,128,512]{3,2,1,0:T(8,128)(2,1)} %field_ref.3, bf16[4,128,512]{2,1,0:T(8,128)(2,1)S(1)} %copy-done.4, ...), custom_call_target="tpu_custom_call" | custom-call | tf_op jit(solution)/shard_map/middle/pallas_call | solution.py:362
  137.2 0.7 copy-done.13
  137.9 1.8 reshape.27
  139.7 1.8 select_reduce_fusion
  141.6 0.7 slice_reduce_fusion
  142.4 0.1 reduce_sum.19
  142.5 66.5 %all-reduce = (f32[20,20]{1,0:T(8,128)}, f32[20]{0:T(128)}) all-reduce(f32[20,20]{1,0:T(8,128)S(1)} %select_reduce_fusion, f32[20]{0:T(128)S(1)} %reduce_sum.19), channel_id=1, replica_groups=mesh['groups'=2,'gx'=16] {'gx'}, use_global_device_ids=true, to_apply=%region_1.2 | all-reduce | flops 420 | bytes 3360 | tf_op jit(solution)/shard_map/psum | solution.py:471
  208.9 2.4 copy-done.2
  211.3 33.1 %adjoint_mix.1 = (bf16[10,192,256]{2,1,0:T(8,128)(2,1)S(1)}, f32[20,48,72]{2,1,0:T(8,128)S(1)}) custom-call(bf16[16,160,72]{2,1,0:T(8,128)(2,1)S(1)} %get-tuple-element.12.sent, bf16[2,20,20,24,72]{4,3,2,1,0:T(8,128)(2,1)S(1)} %copy-done.2, bf16[96,256]{1,0:T(8,128)(2,1)S(1)} %copy-done.12, bf16[256,96]{1,0:T(8,128)(2,1)S(1)} %copy-done.8), custom_call_target="tpu_custom_call" | custom-call | tf_op jit(solution)/shard_map/adjoint_mix/pallas_call | solution.py:251
  244.5 32.3 %last.1 = bf16[20,4,128,512]{3,2,1,0:T(8,128)(2,1)} custom-call(bf16[10,192,256]{2,1,0:T(8,128)(2,1)S(1)} %get-tuple-element.13.rows_ref, bf16[20,4,128,512]{3,2,1,0:T(8,128)(2,1)} %get-tuple-element.14.grad_ref, bf16[160,160]{1,0:T(8,128)(2,1)S(1)} %mul.27.kron_ref, bf16[256,512]{1,0:T(8,128)(2,1)S(1)} %copy-done.7, bf16[4,256,192]{2,1,0:T(8,128)(2,1)S(1)} %copy-done.3), custom_call_target="tpu_custom_call" | custom-call | tf_op jit(solution)/shard_map/last/pallas_call | solution.py:415
  276.8 8.5 %outer.1 = f32[2,20,20,24,72]{4,3,2,1,0:T(8,128)} custom-call(f32[20,48,72]{2,1,0:T(8,128)S(1)} %get-tuple-element.15.spec_ref, f32[20,48,72]{2,1,0:T(8,128)S(1)} %get-tuple-element.16.back_ref), custom_call_target="tpu_custom_call" | custom-call | tf_op jit(solution)/shard_map/outer/pallas_call | solution.py:440
  (34 shorter events, 0.5 us)
Async XLA Ops:
  0.6 4.0 %copy-start = (bf16[20,4,128,512]{3,2,1,0:T(8,128)(2,1)S(1)}, bf16[20,4,128,512]{3,2,1,0:T(8,128)(2,1)}, u32[]{:S(2)}) copy-start(bf16[20,4,128,512]{3,2,1,0:T(8,128)(2,1)} %field_ref.3) | copy-start | bytes 31457284
  4.6 1.0 copy-start.5
  5.6 0.9 copy-start.9
  6.6 8.9 %copy-start.1 = (bf16[2,20,20,24,72]{4,3,2,1,0:T(8,128)(2,1)S(1)}, bf16[2,20,20,24,72]{4,3,2,1,0:T(8,128)(2,1)}, u32[]{:S(2)}) copy-start(bf16[2,20,20,24,72]{4,3,2,1,0:T(8,128)(2,1)} %weight_hbm.3) | copy-start | bytes 8294404
  6.6 8.9 %copy-start.8 = (bf16[256,96]{1,0:T(8,128)(2,1)S(1)}, bf16[256,96]{1,0:T(8,128)(2,1)}, u32[]{:S(2)}) copy-start(bf16[256,96]{1,0:T(8,128)(2,1)} %constant.25.clone.back_ref) | copy-start | bytes 147460
  6.6 8.9 %copy-start.12 = (bf16[96,256]{1,0:T(8,128)(2,1)S(1)}, bf16[96,256]{1,0:T(8,128)(2,1)}, u32[]{:S(2)}) copy-start(bf16[96,256]{1,0:T(8,128)(2,1)} %constant.24.clone.stream_ref) | copy-start | bytes 147460
  15.5 37.1 %copy-start.14 = (bf16[20,20]{1,0:T(8,128)(2,1)S(1)}, bf16[20,20]{1,0:T(8,128)(2,1)}, u32[]{:S(2)}) copy-start(bf16[20,20]{1,0:T(8,128)(2,1)} %param.19) | copy-start | bytes 2404
  15.5 40.1 %copy-start.15 = (f32[20]{0:T(128)S(1)}, f32[20]{0:T(128)}, u32[]{:S(2)}) copy-start(f32[20]{0:T(128)} %param.17) | copy-start | bytes 244
  15.6 40.4 %copy-start.16 = (f32[20]{0:T(128)S(1)}, f32[20]{0:T(128)}, u32[]{:S(2)}) copy-start(f32[20]{0:T(128)} %param.20) | copy-start | bytes 244
  15.6 40.6 %copy-start.3 = (bf16[4,256,192]{2,1,0:T(8,128)(2,1)S(1)}, bf16[4,256,192]{2,1,0:T(8,128)(2,1)}, u32[]{:S(2)}) copy-start(bf16[4,256,192]{2,1,0:T(8,128)(2,1)} %constant.22.clone.lat_inv_ref) | copy-start | bytes 1179652
  15.6 40.6 %copy-start.4 = (bf16[4,128,512]{2,1,0:T(8,128)(2,1)S(1)}, bf16[4,128,512]{2,1,0:T(8,128)(2,1)}, u32[]{:S(2)}) copy-start(bf16[4,128,512]{2,1,0:T(8,128)(2,1)} %sat_ref.1) | copy-start | bytes 1572868
  56.2 1.0 copy-start.6
  57.2 0.9 copy-start.10
  58.2 0.9 copy-start.11
  137.2 0.7 copy-start.13
  137.9 106.6 %copy-start.7 = (bf16[256,512]{1,0:T(8,128)(2,1)S(1)}, bf16[256,512]{1,0:T(8,128)(2,1)}, u32[]{:S(2)}) copy-start(bf16[256,512]{1,0:T(8,128)(2,1)} %constant.29.clone.table_ref) | copy-start | bytes 786436
  208.9 2.4 copy-start.2
where the time goes:
time: 290 us; the launch traced here: 285 us
  Pallas kernels  198 us (68%)
  blocking collectives  66.5 us (23%)
  local copies, waits for them, and re-layouts  16.9 us (6%)
  other arithmetic  3.04 us (1%)
    pallas_call x1, Pallas kernels, middle_call(): pl.pallas_call(partial(middle_kernel, n, rr), grid=(NY // YB,), out_shape...  78.1 us
    pallas_call x2, Pallas kernels, mix_call(): pl.pallas_call(partial(mix_kernel, n, rr, adjoint), out_shape=(jax.ShapeD...  70.2 us
    psum x1, blocking collectives, local(): grad_point, grad_bias = lax.psum((diagonal, bias_part), 'gx')  66.5 us
    pallas_call x1, Pallas kernels, last_call(): pl.pallas_call(last_kernel, grid=(NY // YB,), out_shape=jax.ShapeDtypeStr...  32.3 us
    unnamed x34, local copies, waits for them, and re-layouts  11.9 us
    pallas_call x1, Pallas kernels, forward_call(): pl.pallas_call(partial(forward_kernel, n, rr), grid=(channels // 2,), out...  8.91 us
    pallas_call x1, Pallas kernels, outer_call(): pl.pallas_call(outer_kernel, grid=(channels,), out_shape=jax.ShapeDtypeSt...  8.5 us

commit v1 on v0

--- a/solution.py
+++ b/solution.py
@@ -139,7 +139,7 @@
             pl.BlockSpec(lateral_whole.shape, lambda c: (0, 0)),
         ],
         out_specs=pl.BlockSpec((n, 2 * rr, per), lambda c: (0, c, 0)),
-        compiler_params=params(40),
+        compiler_params=params(60),
         name="forward",
     )(field, plane_table, lateral_whole)
 
@@ -165,10 +165,35 @@
     return copies
 
 
+def spread_parts(n, source, target, send, recv, local):
+    me, group = lax.axis_index("gx"), lax.axis_index("groups")
+    copies = []
+    for k in range(1, n):
+        copy = pltpu.make_async_remote_copy(
+            src_ref=source,
+            dst_ref=target.at[me],
+            send_sem=send.at[k],
+            recv_sem=recv.at[k],
+            device_id=(group, lax.rem(me + k, n)),
+            device_id_type=MESH,
+        )
+        copy.start()
+        copies.append(copy)
+    own = pltpu.make_async_copy(source, target.at[me], local)
+    own.start()
+    own.wait()
+    return copies
+
+
 def mix_kernel(
-    n, rr, adjoint, sent, weight_hbm, stream_ref, back_ref, rows_out, spec_out,
-    got, weights, mixed_wire, got_back, send, recv, local, weight_sem,
+    n, rr, adjoint, sent, weight_hbm, stream_ref, back_ref, *refs
 ):
+    if adjoint:
+        part_ref, rows_out, spec_out, total_ref, *refs = refs
+        *refs, parts, part_send, part_recv, part_local = refs
+    else:
+        rows_out, spec_out, *refs = refs
+    got, weights, mixed_wire, got_back, send, recv, local, weight_sem = refs
     channels = spec_out.shape[0]
     per = spec_out.shape[2]
     me, group = lax.axis_index("gx"), lax.axis_index("groups")
@@ -219,8 +244,17 @@
         )
 
     copies = exchange(n, mixed_wire, got_back, send.at[1], recv.at[1], local.at[1])
+    if adjoint:
+        shares = spread_parts(n, part_ref, parts, part_send, part_recv, part_local)
     for copy in copies:
         copy.wait()
+    if adjoint:
+        for copy in shares:
+            copy.wait()
+        total = parts[0]
+        for d in range(1, n):
+            total = total + parts[d]
+        total_ref[...] = total
 
     pieces_of = mode_pieces(n)
 
@@ -244,39 +278,45 @@
         rows_out[pair] = jnp.concatenate(halves, axis=1).astype(BF)
 
 
-def mix_call(sent, weight, stream, stream_back, n, adjoint):
+def mix_call(sent, weight, stream, stream_back, n, part=None):
     channels = weight.shape[1]
     rr = sent.shape[1] // channels
     per = sent.shape[2]
+    adjoint = part is not None
+    vmem = pl.BlockSpec(memory_space=pltpu.VMEM)
+    out_shape = [
+        jax.ShapeDtypeStruct((channels // 2, KY * rr, 2 * LANES), BF),
+        jax.ShapeDtypeStruct((channels, 2 * KX, per), F32),
+    ]
+    scratch = [
+        pltpu.VMEM(sent.shape, BF),
+        pltpu.VMEM(weight.shape, BF),
+        pltpu.VMEM(sent.shape, BF),
+        pltpu.VMEM(sent.shape, BF),
+        pltpu.SemaphoreType.DMA((2, n)),
+        pltpu.SemaphoreType.DMA((2, n)),
+        pltpu.SemaphoreType.DMA((2,)),
+        pltpu.SemaphoreType.DMA(()),
+    ]
+    operands = [sent, weight, stream, stream_back]
+    if adjoint:
+        out_shape.append(jax.ShapeDtypeStruct(part.shape, F32))
+        scratch += [
+            pltpu.VMEM((n,) + part.shape, F32),
+            pltpu.SemaphoreType.DMA((n,)),
+            pltpu.SemaphoreType.DMA((n,)),
+            pltpu.SemaphoreType.DMA(()),
+        ]
+        operands.append(part)
     return pl.pallas_call(
         partial(mix_kernel, n, rr, adjoint),
-        out_shape=(
-            jax.ShapeDtypeStruct((channels // 2, KY * rr, 2 * LANES), BF),
-            jax.ShapeDtypeStruct((channels, 2 * KX, per), F32),
-        ),
-        in_specs=[
-            pl.BlockSpec(memory_space=pltpu.VMEM),
-            pl.BlockSpec(memory_space=pl.ANY),
-            pl.BlockSpec(memory_space=pltpu.VMEM),
-            pl.BlockSpec(memory_space=pltpu.VMEM),
-        ],
-        out_specs=(
-            pl.BlockSpec(memory_space=pltpu.VMEM),
-            pl.BlockSpec(memory_space=pltpu.VMEM),
-        ),
-        scratch_shapes=[
-            pltpu.VMEM(sent.shape, BF),
-            pltpu.VMEM(weight.shape, BF),
-            pltpu.VMEM(sent.shape, BF),
-            pltpu.VMEM(sent.shape, BF),
-            pltpu.SemaphoreType.DMA((2, n)),
-            pltpu.SemaphoreType.DMA((2, n)),
-            pltpu.SemaphoreType.DMA((2,)),
-            pltpu.SemaphoreType.DMA(()),
-        ],
+        out_shape=out_shape,
+        in_specs=[vmem, pl.BlockSpec(memory_space=pl.ANY)] + [vmem] * (len(operands) - 2),
+        out_specs=[vmem] * len(out_shape),
+        scratch_shapes=scratch,
         compiler_params=params(40, collective_id=int(adjoint), has_side_effects=True),
         name="adjoint_mix" if adjoint else "mix",
-    )(sent, weight, stream, stream_back)
+    )(*operands)
 
 
 def gelu_slope(v):
@@ -290,19 +330,45 @@
     return jnp.where(v >= 0, 1.0 - tail, tail)
 
 
-def planes(rows_ref, lateral, table, store, channels, cells):
-    @pl.loop(0, channels // 2)
+def planes(rows_ref, lateral, table_ref, flat, spectral, channels, cells):
+    @pl.loop(0, channels // 2, unroll=5)
     def _(pair):
-        flat = dot(lateral, rows_ref[pair]).astype(BF)
+        both = dot(lateral, rows_ref[pair]).astype(BF)
         for half in range(2):
             at = slice(half * LANES, (half + 1) * LANES)
-            plane = jnp.concatenate([flat[:cells, at], flat[cells:, at]], axis=1)
-            store(2 * pair + half, dot(plane, table))
+            plane = jnp.concatenate([both[:cells, at], both[cells:, at]], axis=1)
+            flat[pl.ds(pl.multiple_of((2 * pair + half) * cells, cells), cells), :] = plane
+
+    some = 4 * cells
+
+    @pl.loop(0, channels // 4)
+    def _(chunk):
+        here = pl.ds(pl.multiple_of(chunk * some, some), some)
+        out = dot(flat[here, :], table_ref[...])
+        spectral[pl.ds(chunk * 4, 4)] = out.reshape((4,) + spectral.shape[1:])
+
+
+def expand(channels):
+    row = lax.broadcasted_iota(jnp.int32, (channels * 8, channels), 0)
+    column = lax.broadcasted_iota(jnp.int32, (channels * 8, channels), 1)
+    spread = ((row >= column * 8) & (row < column * 8 + 8)).astype(BF)
+    wide = (channels * 8, channels * 8)
+    phase = lax.broadcasted_iota(jnp.int32, wide, 0) - lax.broadcasted_iota(jnp.int32, wide, 1)
+    return spread, lax.rem(phase + channels * 8, 8) == 0
+
+
+def kronecker(weight, channels):
+    spread, mask = expand(channels)
+    wide = lax.dot_general(
+        dot(spread, weight).astype(BF), spread, (((1,), (1,)), ((), ())), preferred_element_type=F32
+    )
+    return jnp.where(mask, wide, 0.0).astype(BF)
 
 
 def middle_kernel(
-    n, rr, rows_ref, field_ref, sat_ref, readout_ref, bias_ref, kron_ref, inverse_ref, back_ref,
-    lat_inv_ref, lat_fwd_ref, grad_ref, wire_ref, corr_ref, spectral, spectrum,
+    n, rr, readout_ref, bias_ref, rows_ref, field_ref, sat_ref, weight_ref, inverse_ref, back_ref,
+    lat_inv_ref, lat_fwd_ref, grad_ref, wire_ref, total_ref,
+    spectral, spectrum, flat, kron, readout_rows, bias_rows, corr,
 ):
     step = pl.program_id(0)
     channels, rows = field_ref.shape[:2]
@@ -310,37 +376,49 @@
 
     @pl.when(step == 0)
     def _():
-        corr_ref[...] = jnp.zeros_like(corr_ref)
+        corr[...] = jnp.zeros_like(corr)
         spectrum[...] = jnp.zeros_like(spectrum)
-
-    def keep(o, value):
-        spectral[o] = value.reshape(rows, YB, NZT)
-
-    planes(rows_ref, lat_inv_ref[0], inverse_ref[...], keep, channels, cells)
+        kron[...] = kronecker(weight_ref[...].astype(F32).T.astype(BF), channels)
+        for o in range(channels):
+            readout_rows[8 * o : 8 * o + 8, :] = jnp.full((8, LANES), readout_ref[o], F32)
+            bias_rows[8 * o : 8 * o + 8, :] = jnp.full((8, LANES), bias_ref[o], F32)
+
+    planes(rows_ref, lat_inv_ref[0], inverse_ref, flat, spectral, channels, cells)
 
     @pl.loop(0, rows)
     def _(x):
-        @pl.loop(0, YB // 8)
-        def _(yb):
-            y8 = pl.ds(pl.multiple_of(yb * 8, 8), 8)
+        lefts, rights = [], []
+        for yb in range(YB // 8):
+            y8 = slice(yb * 8, yb * 8 + 8)
             block = field_ref[:, x, y8, :].reshape(channels * 8, NZT)
-            point = dot(kron_ref[...], block)
-            bias = jnp.concatenate([bias_ref[...]] * (NZT // LANES), axis=1)
-            readout = jnp.concatenate([readout_ref[...]] * (NZT // LANES), axis=1)
+            point = dot(kron[...], block)
+            bias = jnp.concatenate([bias_rows[...]] * (NZT // LANES), axis=1)
+            readout = jnp.concatenate([readout_rows[...]] * (NZT // LANES), axis=1)
             pre = point + spectral[:, x, y8, :].reshape(channels * 8, NZT) + bias
             sat = sat_ref[x, y8, :].astype(F32)
             up = readout * jnp.broadcast_to(sat[None], (channels, 8, NZT)).reshape(-1, NZT)
             grad = (up * gelu_slope(pre)).astype(BF)
             grad_ref[:, x, y8, :] = grad.reshape(channels, 8, NZT)
-            left = jnp.concatenate([block, jnp.ones((16, NZT), BF)], axis=0)
-            corr_ref[...] += lax.dot_general(
-                left, grad, (((1,), (1,)), ((), ())), preferred_element_type=F32
-            )
-
-    @pl.loop(0, channels // 2)
+            lefts.append(jnp.concatenate([block, jnp.ones((16, NZT), BF)], axis=0))
+            rights.append(grad)
+        corr[...] += lax.dot_general(
+            jnp.concatenate(lefts, axis=1),
+            jnp.concatenate(rights, axis=1),
+            (((1,), (1,)), ((), ())),
+            preferred_element_type=F32,
+        )
+
+    some = 4 * cells
+
+    @pl.loop(0, channels // 4)
+    def _(chunk):
+        grads = grad_ref[pl.ds(chunk * 4, 4)].reshape(some, NZT)
+        flat[pl.ds(pl.multiple_of(chunk * some, some), some), :] = dot(grads, back_ref[...]).astype(BF)
+
+    @pl.loop(0, channels // 2, unroll=5)
     def _(pair):
         flats = [
-            dot(grad_ref[2 * pair + half].reshape(cells, NZT), back_ref[...]).astype(BF)
+            flat[pl.ds(pl.multiple_of((2 * pair + half) * cells, cells), cells), :]
             for half in range(2)
         ]
         real = jnp.concatenate([f[:, :LANES] for f in flats], axis=1)
@@ -353,102 +431,128 @@
         def _(pair):
             pack(spectrum[pair], wire_ref, pl.multiple_of(pair * 2 * rr, 16), n, rr)
 
-
-def middle_call(rows_in, field, sat, readout, bias, kron, inverse, back, lat_inv, lat_fwd, n):
+        spread, mask = expand(channels)
+        spread = spread.astype(F32)
+        best = partial(
+            lax.dot_general, preferred_element_type=F32, precision=lax.Precision.HIGHEST
+        )
+        sums = jnp.where(mask, corr[: channels * 8], 0.0)
+        inner = best(sums, spread, (((1,), (0,)), ((), ())))
+        total_ref[:channels, :] = best(spread, inner, (((0,), (0,)), ((), ())))
+        total_ref[channels : channels + 4, :] = best(
+            corr[channels * 8 : channels * 8 + 4], spread, (((1,), (0,)), ((), ()))
+        )
+
+
+def middle_call(rows_in, field, sat, readout, bias, weight, inverse, back, lat_inv, lat_fwd, n):
     channels, rows = field.shape[:2]
     rr = 2 * rows
     per = KY * KZT // n
     whole = lambda a: pl.BlockSpec(a.shape, lambda y: (0,) * a.ndim)
+    scalars = pl.BlockSpec(memory_space=pltpu.SMEM)
     return pl.pallas_call(
         partial(middle_kernel, n, rr),
         grid=(NY // YB,),
         out_shape=(
             jax.ShapeDtypeStruct(field.shape, BF),
             jax.ShapeDtypeStruct((n, channels * rr, per), BF),
-            jax.ShapeDtypeStruct((channels * 8 + 16, channels * 8), F32),
+            jax.ShapeDtypeStruct((channels + 4, channels), F32),
         ),
         in_specs=[
+            scalars, scalars,
             whole(rows_in),
             pl.BlockSpec((channels, rows, YB, NZT), lambda y: (0, 0, y, 0)),
             pl.BlockSpec((rows, YB, NZT), lambda y: (0, y, 0)),
-            whole(readout), whole(bias), whole(kron), whole(inverse), whole(back),
+            whole(weight), whole(inverse), whole(back),
             pl.BlockSpec((1,) + lat_inv.shape[1:], lambda y: (y, 0, 0)),
             pl.BlockSpec((1,) + lat_fwd.shape[1:], lambda y: (y, 0, 0)),
         ],
         out_specs=(
             pl.BlockSpec((channels, rows, YB, NZT), lambda y: (0, 0, y, 0)),
             pl.BlockSpec((n, channels * rr, per), lambda y: (0, 0, 0)),
-            pl.BlockSpec((channels * 8 + 16, channels * 8), lambda y: (0, 0)),
+            pl.BlockSpec((channels + 4, channels), lambda y: (0, 0)),
         ),
         scratch_shapes=[
             pltpu.VMEM((channels, rows, YB, NZT), F32),
             pltpu.VMEM((channels // 2, KY * rr, 2 * LANES), F32),
+            pltpu.VMEM((channels * rows * YB, 2 * LANES), BF),
+            pltpu.VMEM((channels * 8, channels * 8), BF),
+            pltpu.VMEM((channels * 8, LANES), F32),
+            pltpu.VMEM((channels * 8, LANES), F32),
+            pltpu.VMEM((channels * 8 + 16, channels * 8), F32),
         ],
-        compiler_params=params(48),
+        compiler_params=params(58),
         name="middle",
-    )(rows_in, field, sat, readout, bias, kron, inverse, back, lat_inv, lat_fwd)
-
-
-def last_kernel(rows_ref, grad_ref, kron_ref, table_ref, lat_inv_ref, out_ref, spectral):
+    )(readout, bias, rows_in, field, sat, weight, inverse, back, lat_inv, lat_fwd)
+
+
+def last_kernel(
+    rows_ref, grad_ref, weight_ref, table_ref, lat_inv_ref, spec_ref, back_ref, total_ref,
+    out_ref, outer_ref, point_ref, bias_ref, spectral, flat, kron,
+):
     channels, rows = grad_ref.shape[:2]
     cells = rows * YB
 
-    def keep(o, value):
-        spectral[o] = value.reshape(rows, YB, NZT)
-
-    planes(rows_ref, lat_inv_ref[0], table_ref[...], keep, channels, cells)
+    @pl.when(pl.program_id(0) == 0)
+    def _():
+        kron[...] = kronecker(weight_ref[...], channels)
+        point_ref[...] = total_ref[:channels, :]
+        bias_ref[...] = total_ref[channels : channels + 1, :]
+
+    planes(rows_ref, lat_inv_ref[0], table_ref, flat, spectral, channels, cells)
 
     @pl.loop(0, rows)
     def _(x):
-        @pl.loop(0, YB // 8)
-        def _(yb):
-            y8 = pl.ds(pl.multiple_of(yb * 8, 8), 8)
+        for yb in range(YB // 8):
+            y8 = slice(yb * 8, yb * 8 + 8)
             block = grad_ref[:, x, y8, :].reshape(channels * 8, NZT)
-            total = dot(kron_ref[...], block) + spectral[:, x, y8, :].reshape(channels * 8, NZT)
+            total = dot(kron[...], block) + spectral[:, x, y8, :].reshape(channels * 8, NZT)
             out_ref[:, x, y8, :] = total.astype(BF).reshape(channels, 8, NZT)
 
-
-def last_call(rows_in, grad, kron, table, lat_inv):
+    @pl.loop(0, outer_ref.shape[1])
+    def _(i):
+        s_real, s_imag = spec_ref[i, :KX], spec_ref[i, KX:]
+        for o in range(channels):
+            b_real, b_imag = back_ref[o, :KX], back_ref[o, KX:]
+            outer_ref[0, i, o] = s_real * b_real + s_imag * b_imag
+            outer_ref[1, i, o] = s_real * b_imag - s_imag * b_real
+
+
+def last_call(rows_in, grad, weight, table, lat_inv, spec, back_spec, total):
     channels, rows = grad.shape[:2]
+    per = spec.shape[2]
+    steps = NY // YB
     whole = lambda a: pl.BlockSpec(a.shape, lambda y: (0,) * a.ndim)
     block = pl.BlockSpec((channels, rows, YB, NZT), lambda y: (0, 0, y, 0))
     return pl.pallas_call(
         last_kernel,
-        grid=(NY // YB,),
-        out_shape=jax.ShapeDtypeStruct(grad.shape, BF),
+        grid=(steps,),
+        out_shape=(
+            jax.ShapeDtypeStruct(grad.shape, BF),
+            jax.ShapeDtypeStruct((2, channels, channels, KX, per), F32),
+            jax.ShapeDtypeStruct((channels, channels), F32),
+            jax.ShapeDtypeStruct((1, channels), F32),
+        ),
         in_specs=[
-            whole(rows_in), block, whole(kron), whole(table),
+            whole(rows_in), block, whole(weight), whole(table),
             pl.BlockSpec((1,) + lat_inv.shape[1:], lambda y: (y, 0, 0)),
+            pl.BlockSpec((channels // steps,) + spec.shape[1:], lambda y: (y, 0, 0)),
+            whole(back_spec), whole(total),
         ],
-        out_specs=block,
-        scratch_shapes=[pltpu.VMEM((channels, rows, YB, NZT), F32)],
-        compiler_params=params(48),
+        out_specs=(
+            block,
+            pl.BlockSpec((2, channels // steps, channels, KX, per), lambda y: (0, y, 0, 0, 0)),
+            pl.BlockSpec((channels, channels), lambda y: (0, 0)),
+            pl.BlockSpec((1, channels), lambda y: (0, 0)),
+        ),
+        scratch_shapes=[
+            pltpu.VMEM((channels, rows, YB, NZT), F32),
+            pltpu.VMEM((channels * rows * YB, 2 * LANES), BF),
+            pltpu.VMEM((channels * 8, channels * 8), BF),
+        ],
+        compiler_params=params(58),
         name="last",
-    )(rows_in, grad, kron, table, lat_inv)
-
-
-def outer_kernel(spec_ref, back_ref, out_ref):
-    s_real, s_imag = spec_ref[0, :KX], spec_ref[0, KX:]
-    for o in range(back_ref.shape[0]):
-        b_real, b_imag = back_ref[o, :KX], back_ref[o, KX:]
-        out_ref[0, 0, o] = s_real * b_real + s_imag * b_imag
-        out_ref[1, 0, o] = s_real * b_imag - s_imag * b_real
-
-
-def outer_call(spec, back):
-    channels, _, per = spec.shape
-    return pl.pallas_call(
-        outer_kernel,
-        grid=(channels,),
-        out_shape=jax.ShapeDtypeStruct((2, channels, channels, KX, per), F32),
-        in_specs=[
-            pl.BlockSpec((1, 2 * KX, per), lambda i: (i, 0, 0)),
-            pl.BlockSpec(back.shape, lambda i: (0, 0, 0)),
-        ],
-        out_specs=pl.BlockSpec((2, 1, channels, KX, per), lambda i: (0, i, 0, 0, 0)),
-        compiler_params=params(24),
-        name="outer",
-    )(spec, back)
+    )(rows_in, grad, weight, table, lat_inv, spec, back_spec, total)
 
 
 def local(n, lifted_field, saturation_grad, readout, spectral_weight, point_weight, point_bias):
@@ -456,23 +560,18 @@
     forward_table, inverse_table = plane_tables()
     lat_fwd, lat_inv, lat_whole = lateral_tables(rows)
     stream, stream_back = stream_tables(rows * n, rows)
-    eye = jnp.eye(8, dtype=BF)
-    kron = jnp.kron(point_weight, eye)
-    spread = lambda a: jnp.broadcast_to(jnp.repeat(a, 8)[:, None], (channels * 8, LANES))
 
     sent = forward_call(lifted_field, narrow(forward_table), lat_whole, n)
-    rows_in, spec = mix_call(sent, spectral_weight, stream, stream_back, n, False)
-    grad_pre, sent_back, corr = middle_call(
-        rows_in, lifted_field, saturation_grad, spread(readout), spread(point_bias), kron.T,
+    rows_in, spec = mix_call(sent, spectral_weight, stream, stream_back, n)
+    grad_pre, sent_back, part = middle_call(
+        rows_in, lifted_field, saturation_grad, readout, point_bias, point_weight,
         narrow(inverse_table.T), narrow(inverse_table), lat_inv, lat_fwd, n,
     )
-    diagonal = jnp.einsum("iaoa->io", corr[: channels * 8].reshape(channels, 8, channels, 8))
-    bias_part = corr[channels * 8].reshape(channels, 8).sum(axis=1)
-    grad_point, grad_bias = lax.psum((diagonal, bias_part), "gx")
-    rows_back, back_spec = mix_call(sent_back, spectral_weight, stream, stream_back, n, True)
-    grad_spectral = outer_call(spec, back_spec)
-    grad_field = last_call(rows_back, grad_pre, kron, narrow(forward_table.T), lat_inv)
-    return (grad_field, grad_spectral, grad_point, grad_bias)
+    rows_back, back_spec, total = mix_call(sent_back, spectral_weight, stream, stream_back, n, part)
+    grad_field, grad_spectral, grad_point, grad_bias = last_call(
+        rows_back, grad_pre, point_weight, narrow(forward_table.T), lat_inv, spec, back_spec, total
+    )
+    return (grad_field, grad_spectral, grad_point, grad_bias.reshape(channels))
 
 
 def solution(mesh):

time: 290 us -> 179 us (0.62); the launches traced: 285 us -> 178 us
  blocking collectives: 66.5 us -> 0 us
  Pallas kernels: 198 us -> 168 us
  local copies, waits for them, and re-layouts: 16.9 us -> 9.36 us
  other arithmetic: 3.04 us -> 0.01 us
    psum x1 -> x0, blocking collectives: 66.5 us -> none  [local(): grad_point, grad_bias = lax.psum((diagonal, bias_part), 'gx')]
    pallas_call x1, Pallas kernels: 78.1 us -> 49.3 us  [middle_call(): pl.pallas_call(partial(middle_kernel, n, rr), grid=(NY // YB,), out_shape...]
    pallas_call x4 -> x3, Pallas kernels: 111 us -> 106 us  [the longest x2 85.9 us: mix_call(): pl.pallas_call(partial(mix_kernel, n, rr, adjoint), out_shape=out_shape,...]
    pallas_call x1, Pallas kernels: 8.91 us -> 12.7 us  [forward_call(): pl.pallas_call(partial(forward_kernel, n, rr), grid=(channels // 2,), out...]
    unnamed x34 -> x26, local copies, waits for them, and re-layouts: 11.9 us -> 9.36 us
where the time goes in v1:
time: 179 us; the launch traced here: 178 us
  Pallas kernels  168 us (94%)
  local copies, waits for them, and re-layouts  9.36 us (5%)
    pallas_call x2, Pallas kernels, mix_call(): pl.pallas_call(partial(mix_kernel, n, rr, adjoint), out_shape=out_shape,...  85.9 us
    pallas_call x1, Pallas kernels, middle_call(): pl.pallas_call(partial(middle_kernel, n, rr), grid=(NY // YB,), out_shape...  49.3 us
    pallas_call x1, Pallas kernels, last_call(): pl.pallas_call(last_kernel, grid=(steps,), out_shape=(jax.ShapeDtypeStruc...  20.1 us
    pallas_call x1, Pallas kernels, forward_call(): pl.pallas_call(partial(forward_kernel, n, rr), grid=(channels // 2,), out...  12.7 us
    unnamed x26, local copies, waits for them, and re-layouts  9.36 us

profile of v1, /device:TPU:0, one launch (start us, length us, event | category | flops | bytes accessed | tf_op | source)
XLA Modules:
  0.0 178.1 jit_solution(14822671713580565168)
XLA Ops:
  0.6 0.0 copy-start.7
  0.6 0.0 copy-start.8
  0.7 12.7 %forward.1.sent = bf16[16,160,72]{2,1,0:T(8,128)(2,1)} custom-call(bf16[20,4,128,512]{3,2,1,0:T(8,128)(2,1)} %field_ref.3, bf16[512,256]{1,0:T(8,128)(2,1)} %constant.23.clone.plane_ref, bf16[192,1024]{1,0:T(8,128)(2,1)} %constant.20.clone.lateral_ref), custom_call_target="tpu_custom_call" | custom-call | tf_op jit(solution)/shard_map/forward/pallas_call | solution.py:132
  13.3 0.0 copy-done.7
  13.3 0.0 copy-done.8
  13.3 0.0 copy-start
  13.4 2.4 %copy-done = bf16[2,20,20,24,72]{4,3,2,1,0:T(8,128)(2,1)S(1)} copy-done((bf16[2,20,20,24,72]{4,3,2,1,0:T(8,128)(2,1)S(1)}, bf16[2,20,20,24,72]{4,3,2,1,0:T(8,128)(2,1)}, u32[]{:S(2)}) %copy-start) | copy-done | bytes 2764824
  15.7 1.1 copy-done.1
  16.8 36.9 %mix.1 = (bf16[10,192,256]{2,1,0:T(8,128)(2,1)S(1)}, f32[20,48,72]{2,1,0:T(8,128)S(1)}) custom-call(bf16[16,160,72]{2,1,0:T(8,128)(2,1)S(1)} %copy-done.1, bf16[2,20,20,24,72]{4,3,2,1,0:T(8,128)(2,1)S(1)} %copy-done, bf16[96,256]{1,0:T(8,128)(2,1)S(1)} %copy-done.8, bf16[256,96]{1,0:T(8,128)(2,1)S(1)} %copy-done.7), custom_call_target="tpu_custom_call" | custom-call | tf_op jit(solution)/shard_map/mix/pallas_call | solution.py:311
  53.8 0.0 copy-start.3
  53.8 0.9 copy-done.3
  54.7 0.8 copy-done.5
  55.5 49.3 %middle.1 = (bf16[20,4,128,512]{3,2,1,0:T(8,128)(2,1)}, bf16[16,160,72]{2,1,0:T(8,128)(2,1)}, f32[24,20]{1,0:T(8,128)}) custom-call(f32[20]{0:T(128)} %readout_ref.1, f32[20]{0:T(128)} %bias_ref.1, bf16[10,192,256]{2,1,0:T(8,128)(2,1)} %copy-done.3, bf16[20,4,128,512]{3,2,1,0:T(8,128)(2,1)} %field_ref.3, bf16[4,128,512]{2,1,0:T(8,128)(2,1)} %sat_ref.1, ...), custom_call_target="tpu_custom_call" | custom-call | tf_op jit(solution)/shard_map/middle/pallas_call | solution.py:453
  104.8 0.0 slice-done
  104.8 0.0 slice-done.1
  104.8 0.0 copy-start.4
  104.8 1.1 copy-done.4
  105.9 0.7 copy-done.10
  106.6 48.9 %adjoint_mix.1 = (bf16[10,192,256]{2,1,0:T(8,128)(2,1)S(1)}, f32[20,48,72]{2,1,0:T(8,128)S(1)}, f32[24,20]{1,0:T(8,128)S(1)}) custom-call(bf16[16,160,72]{2,1,0:T(8,128)(2,1)S(1)} %copy-done.4, bf16[2,20,20,24,72]{4,3,2,1,0:T(8,128)(2,1)S(1)} %bitcast.2, bf16[96,256]{1,0:T(8,128)(2,1)S(1)} %copy-done.8, bf16[256,96]{1,0:T(8,128)(2,1)S(1)} %copy-done.7, ...), custom_call_target="tpu_custom_call" | custom-call | tf_op jit(solution)/shard_map/adjoint_mix/pallas_call | solution.py:311
  155.6 0.0 copy-start.2
  155.6 1.0 copy-done.2
  156.5 0.8 copy-done.6
  157.3 0.6 copy-done.9
  157.9 20.1 %last.1 = (bf16[20,4,128,512]{3,2,1,0:T(8,128)(2,1)}, f32[2,20,20,24,72]{4,3,2,1,0:T(8,128)}, f32[20,20]{1,0:T(8,128)}, f32[1,20]{1,0:T(1,128)}) custom-call(bf16[10,192,256]{2,1,0:T(8,128)(2,1)} %copy-done.2, bf16[20,4,128,512]{3,2,1,0:T(8,128)(2,1)} %get-tuple-element.20.grad_ref, bf16[20,20]{1,0:T(8,128)(2,1)} %weight_ref.3, ...), custom_call_target="tpu_custom_call" | custom-call | tf_op jit(solution)/shard_map/last/pallas_call | solution.py:527
  (8 shorter events, 0.0 us)
Async XLA Ops:
  0.6 12.7 %copy-start.7 = (bf16[256,96]{1,0:T(8,128)(2,1)S(1)}, bf16[256,96]{1,0:T(8,128)(2,1)}, u32[]{:S(2)}) copy-start(bf16[256,96]{1,0:T(8,128)(2,1)} %constant.22.clone.back_ref) | copy-start | bytes 147460
  0.6 12.7 %copy-start.8 = (bf16[96,256]{1,0:T(8,128)(2,1)S(1)}, bf16[96,256]{1,0:T(8,128)(2,1)}, u32[]{:S(2)}) copy-start(bf16[96,256]{1,0:T(8,128)(2,1)} %constant.21.clone.stream_ref) | copy-start | bytes 147460
  13.3 2.4 %copy-start = (bf16[2,20,20,24,72]{4,3,2,1,0:T(8,128)(2,1)S(1)}, bf16[2,20,20,24,72]{4,3,2,1,0:T(8,128)(2,1)}, u32[]{:S(2)}) copy-start(bf16[2,20,20,24,72]{4,3,2,1,0:T(8,128)(2,1)} %weight_hbm.3) | copy-start | bytes 8294404
  15.7 1.1 copy-start.1
  16.8 88.0 %slice-start = ((s8[4915200]{0:T(1024)(128)(4,1)}), s8[4194304]{0:T(1024)(128)(4,1)S(1)}, s32[]{:S(2)}) async-start(s8[4915200]{0:T(1024)(128)(4,1)} %bitcast.1), calls=%async_computation | async-start | bytes 8388608
  53.8 0.9 copy-start.3
  54.7 0.8 copy-start.5
  55.5 49.3 %slice-start.1 = ((s8[4915200]{0:T(1024)(128)(4,1)}), s8[720896]{0:T(1024)(128)(4,1)S(1)}, s32[]{:S(2)}) async-start(s8[4915200]{0:T(1024)(128)(4,1)} %bitcast.1), calls=%async_computation.1 | async-start | bytes 1441792
  104.8 1.1 copy-start.4
  105.9 0.7 copy-start.10
  155.6 1.0 copy-start.2
  156.5 0.8 copy-start.6
  157.3 0.6 copy-start.9

commit v2 on v1

--- a/solution.py
+++ b/solution.py
@@ -186,14 +186,15 @@
 
 
 def mix_kernel(
-    n, rr, adjoint, sent, weight_hbm, stream_ref, back_ref, *refs
+    n, rr, adjoint, sent, weight_hbm, field_hbm, stream_ref, back_ref, point_ref, *refs
 ):
     if adjoint:
-        part_ref, rows_out, spec_out, total_ref, *refs = refs
+        part_ref, rows_out, spec_out, mixed_hbm, total_ref, *refs = refs
         *refs, parts, part_send, part_recv, part_local = refs
     else:
-        rows_out, spec_out, *refs = refs
-    got, weights, mixed_wire, got_back, send, recv, local, weight_sem = refs
+        rows_out, spec_out, mixed_hbm, *refs = refs
+    got, weights, mixed_wire, got_back, kron, send, recv, local, weight_sem = refs
+    rows = field_hbm.shape[1]
     channels = spec_out.shape[0]
     per = spec_out.shape[2]
     me, group = lax.axis_index("gx"), lax.axis_index("groups")
@@ -206,6 +207,9 @@
     fetch.start()
     pl.semaphore_wait(barrier, n - 1)
     copies = exchange(n, sent, got, send.at[0], recv.at[0], local.at[0])
+    point = point_ref[...] if adjoint else point_ref[...].astype(F32).T.astype(BF)
+    kron[...] = kronecker(point, channels)
+    pointwise(kron, field_hbm, mixed_hbm, 0, rows // 2)
     for copy in copies:
         copy.wait()
 
@@ -246,6 +250,7 @@
     copies = exchange(n, mixed_wire, got_back, send.at[1], recv.at[1], local.at[1])
     if adjoint:
         shares = spread_parts(n, part_ref, parts, part_send, part_recv, part_local)
+    pointwise(kron, field_hbm, mixed_hbm, rows // 2, rows - rows // 2)
     for copy in copies:
         copy.wait()
     if adjoint:
@@ -278,7 +283,7 @@
         rows_out[pair] = jnp.concatenate(halves, axis=1).astype(BF)
 
 
-def mix_call(sent, weight, stream, stream_back, n, part=None):
+def mix_call(sent, weight, field, stream, stream_back, point, n, part=None):
     channels = weight.shape[1]
     rr = sent.shape[1] // channels
     per = sent.shape[2]
@@ -287,18 +292,21 @@
     out_shape = [
         jax.ShapeDtypeStruct((channels // 2, KY * rr, 2 * LANES), BF),
         jax.ShapeDtypeStruct((channels, 2 * KX, per), F32),
+        jax.ShapeDtypeStruct(field.shape, BF),
     ]
+    hbm = pl.BlockSpec(memory_space=pl.ANY)
     scratch = [
         pltpu.VMEM(sent.shape, BF),
         pltpu.VMEM(weight.shape, BF),
         pltpu.VMEM(sent.shape, BF),
         pltpu.VMEM(sent.shape, BF),
+        pltpu.VMEM((channels * 8, channels * 8), BF),
         pltpu.SemaphoreType.DMA((2, n)),
         pltpu.SemaphoreType.DMA((2, n)),
         pltpu.SemaphoreType.DMA((2,)),
         pltpu.SemaphoreType.DMA(()),
     ]
-    operands = [sent, weight, stream, stream_back]
+    operands = [sent, weight, field, stream, stream_back, point]
     if adjoint:
         out_shape.append(jax.ShapeDtypeStruct(part.shape, F32))
         scratch += [
@@ -311,26 +319,20 @@
     return pl.pallas_call(
         partial(mix_kernel, n, rr, adjoint),
         out_shape=out_shape,
-        in_specs=[vmem, pl.BlockSpec(memory_space=pl.ANY)] + [vmem] * (len(operands) - 2),
-        out_specs=[vmem] * len(out_shape),
+        in_specs=[vmem, hbm, hbm] + [vmem] * (len(operands) - 3),
+        out_specs=[vmem, vmem, hbm] + [vmem] * (len(out_shape) - 3),
         scratch_shapes=scratch,
-        compiler_params=params(40, collective_id=int(adjoint), has_side_effects=True),
+        compiler_params=params(58, collective_id=int(adjoint), has_side_effects=True),
         name="adjoint_mix" if adjoint else "mix",
     )(*operands)
 
 
 def gelu_slope(v):
-    a = jnp.abs(v)
-    t = 1.0 / (1.0 + (0.3275911 * 0.7071067811865476) * a)
-    e = jnp.exp(-0.5 * v * v)
-    poly = 0.5 * 1.061405429
-    for coefficient in (-1.453152027, 1.421413741, -0.284496736, 0.254829592):
-        poly = poly * t + 0.5 * coefficient
-    tail = e * (poly * t - 0.3989422804014327 * a)
-    return jnp.where(v >= 0, 1.0 - tail, tail)
-
-
-def planes(rows_ref, lateral, table_ref, flat, spectral, channels, cells):
+    cumulative = 0.5 + 0.5 * lax.erf(v * 0.7071067811865476)
+    return cumulative + v * (jnp.exp(-0.5 * v * v) * 0.3989422804014327)
+
+
+def planes(rows_ref, lateral, flat, channels, cells):
     @pl.loop(0, channels // 2, unroll=5)
     def _(pair):
         both = dot(lateral, rows_ref[pair]).astype(BF)
@@ -339,13 +341,20 @@
             plane = jnp.concatenate([both[:cells, at], both[cells:, at]], axis=1)
             flat[pl.ds(pl.multiple_of((2 * pair + half) * cells, cells), cells), :] = plane
 
-    some = 4 * cells
-
-    @pl.loop(0, channels // 4)
-    def _(chunk):
-        here = pl.ds(pl.multiple_of(chunk * some, some), some)
-        out = dot(flat[here, :], table_ref[...])
-        spectral[pl.ds(chunk * 4, 4)] = out.reshape((4,) + spectral.shape[1:])
+
+def pointwise(kron, source, target, first, count):
+    channels = source.shape[0]
+
+    def body(block_ref, out_ref):
+        for yb in range(YB // 8):
+            y8 = slice(yb * 8, yb * 8 + 8)
+            block = block_ref[:, 0, y8, :].reshape(channels * 8, NZT)
+            out_ref[:, 0, y8, :] = dot(kron[...], block).astype(BF).reshape(channels, 8, NZT)
+
+    spec = pl.BlockSpec((channels, 1, YB, NZT), lambda x, y: (0, first + x, y, 0))
+    pltpu.emit_pipeline(body, grid=(count, NY // YB), in_specs=[spec], out_specs=[spec])(
+        source, target
+    )
 
 
 def expand(channels):
@@ -366,9 +375,8 @@
 
 
 def middle_kernel(
-    n, rr, readout_ref, bias_ref, rows_ref, field_ref, sat_ref, weight_ref, inverse_ref, back_ref,
-    lat_inv_ref, lat_fwd_ref, grad_ref, wire_ref, total_ref,
-    spectral, spectrum, flat, kron, readout_rows, bias_rows, corr,
+    n, rr, readout_ref, bias_ref, rows_ref, field_ref, point_ref, sat_ref, inverse_ref, back_ref,
+    lat_inv_ref, lat_fwd_ref, grad_ref, wire_ref, total_ref, spectrum, flat, corr,
 ):
     step = pl.program_id(0)
     channels, rows = field_ref.shape[:2]
@@ -378,12 +386,20 @@
     def _():
         corr[...] = jnp.zeros_like(corr)
         spectrum[...] = jnp.zeros_like(spectrum)
-        kron[...] = kronecker(weight_ref[...].astype(F32).T.astype(BF), channels)
-        for o in range(channels):
-            readout_rows[8 * o : 8 * o + 8, :] = jnp.full((8, LANES), readout_ref[o], F32)
-            bias_rows[8 * o : 8 * o + 8, :] = jnp.full((8, LANES), bias_ref[o], F32)
-
-    planes(rows_ref, lat_inv_ref[0], inverse_ref, flat, spectral, channels, cells)
+
+    planes(rows_ref, lat_inv_ref[0], flat, channels, cells)
+
+    @pl.loop(0, channels // 2)
+    def _(pair):
+        here = pl.ds(pl.multiple_of(pair * 2 * cells, 2 * cells), 2 * cells)
+        both = dot(flat[here, :], inverse_ref[...])
+        sat = sat_ref[...].reshape(cells, NZT).astype(F32)
+        for half in range(2):
+            o = 2 * pair + half
+            pre = both[half * cells : (half + 1) * cells]
+            pre = pre + point_ref[o].reshape(cells, NZT).astype(F32) + bias_ref[o]
+            grad = (readout_ref[o] * sat * gelu_slope(pre)).astype(BF)
+            grad_ref[o] = grad.reshape(rows, YB, NZT)
 
     @pl.loop(0, rows)
     def _(x):
@@ -391,16 +407,8 @@
         for yb in range(YB // 8):
             y8 = slice(yb * 8, yb * 8 + 8)
             block = field_ref[:, x, y8, :].reshape(channels * 8, NZT)
-            point = dot(kron[...], block)
-            bias = jnp.concatenate([bias_rows[...]] * (NZT // LANES), axis=1)
-            readout = jnp.concatenate([readout_rows[...]] * (NZT // LANES), axis=1)
-            pre = point + spectral[:, x, y8, :].reshape(channels * 8, NZT) + bias
-            sat = sat_ref[x, y8, :].astype(F32)
-            up = readout * jnp.broadcast_to(sat[None], (channels, 8, NZT)).reshape(-1, NZT)
-            grad = (up * gelu_slope(pre)).astype(BF)
-            grad_ref[:, x, y8, :] = grad.reshape(channels, 8, NZT)
             lefts.append(jnp.concatenate([block, jnp.ones((16, NZT), BF)], axis=0))
-            rights.append(grad)
+            rights.append(grad_ref[:, x, y8, :].reshape(channels * 8, NZT))
         corr[...] += lax.dot_general(
             jnp.concatenate(lefts, axis=1),
             jnp.concatenate(rights, axis=1),
@@ -438,13 +446,14 @@
         )
         sums = jnp.where(mask, corr[: channels * 8], 0.0)
         inner = best(sums, spread, (((1,), (0,)), ((), ())))
-        total_ref[:channels, :] = best(spread, inner, (((0,), (0,)), ((), ())))
-        total_ref[channels : channels + 4, :] = best(
+        total_ref[...] = jnp.zeros_like(total_ref)
+        total_ref[:channels, :channels] = best(spread, inner, (((0,), (0,)), ((), ())))
+        total_ref[channels : channels + 4, :channels] = best(
             corr[channels * 8 : channels * 8 + 4], spread, (((1,), (0,)), ((), ()))
         )
 
 
-def middle_call(rows_in, field, sat, readout, bias, weight, inverse, back, lat_inv, lat_fwd, n):
+def middle_call(rows_in, field, point, sat, readout, bias, inverse, back, lat_inv, lat_fwd, n):
     channels, rows = field.shape[:2]
     rr = 2 * rows
     per = KY * KZT // n
@@ -456,58 +465,53 @@
         out_shape=(
             jax.ShapeDtypeStruct(field.shape, BF),
             jax.ShapeDtypeStruct((n, channels * rr, per), BF),
-            jax.ShapeDtypeStruct((channels + 4, channels), F32),
+            jax.ShapeDtypeStruct((channels + 4, LANES), F32),
         ),
         in_specs=[
             scalars, scalars,
             whole(rows_in),
             pl.BlockSpec((channels, rows, YB, NZT), lambda y: (0, 0, y, 0)),
+            pl.BlockSpec((channels, rows, YB, NZT), lambda y: (0, 0, y, 0)),
             pl.BlockSpec((rows, YB, NZT), lambda y: (0, y, 0)),
-            whole(weight), whole(inverse), whole(back),
+            whole(inverse), whole(back),
             pl.BlockSpec((1,) + lat_inv.shape[1:], lambda y: (y, 0, 0)),
             pl.BlockSpec((1,) + lat_fwd.shape[1:], lambda y: (y, 0, 0)),
         ],
         out_specs=(
             pl.BlockSpec((channels, rows, YB, NZT), lambda y: (0, 0, y, 0)),
             pl.BlockSpec((n, channels * rr, per), lambda y: (0, 0, 0)),
-            pl.BlockSpec((channels + 4, channels), lambda y: (0, 0)),
+            pl.BlockSpec((channels + 4, LANES), lambda y: (0, 0)),
         ),
         scratch_shapes=[
-            pltpu.VMEM((channels, rows, YB, NZT), F32),
             pltpu.VMEM((channels // 2, KY * rr, 2 * LANES), F32),
             pltpu.VMEM((channels * rows * YB, 2 * LANES), BF),
-            pltpu.VMEM((channels * 8, channels * 8), BF),
-            pltpu.VMEM((channels * 8, LANES), F32),
-            pltpu.VMEM((channels * 8, LANES), F32),
             pltpu.VMEM((channels * 8 + 16, channels * 8), F32),
         ],
         compiler_params=params(58),
         name="middle",
-    )(readout, bias, rows_in, field, sat, weight, inverse, back, lat_inv, lat_fwd)
+    )(readout, bias, rows_in, field, point, sat, inverse, back, lat_inv, lat_fwd)
 
 
 def last_kernel(
-    rows_ref, grad_ref, weight_ref, table_ref, lat_inv_ref, spec_ref, back_ref, total_ref,
-    out_ref, outer_ref, point_ref, bias_ref, spectral, flat, kron,
+    rows_ref, grad_ref, table_ref, lat_inv_ref, spec_ref, back_ref, total_ref,
+    out_ref, outer_ref, point_ref, bias_ref, flat,
 ):
     channels, rows = grad_ref.shape[:2]
     cells = rows * YB
 
     @pl.when(pl.program_id(0) == 0)
     def _():
-        kron[...] = kronecker(weight_ref[...], channels)
-        point_ref[...] = total_ref[:channels, :]
-        bias_ref[...] = total_ref[channels : channels + 1, :]
-
-    planes(rows_ref, lat_inv_ref[0], table_ref, flat, spectral, channels, cells)
-
-    @pl.loop(0, rows)
-    def _(x):
-        for yb in range(YB // 8):
-            y8 = slice(yb * 8, yb * 8 + 8)
-            block = grad_ref[:, x, y8, :].reshape(channels * 8, NZT)
-            total = dot(kron[...], block) + spectral[:, x, y8, :].reshape(channels * 8, NZT)
-            out_ref[:, x, y8, :] = total.astype(BF).reshape(channels, 8, NZT)
+        point_ref[...] = total_ref[:channels, :channels]
+        bias_ref[...] = total_ref[channels : channels + 1, :channels]
+
+    planes(rows_ref, lat_inv_ref[0], flat, channels, cells)
+
+    @pl.loop(0, channels // 4)
+    def _(chunk):
+        here = pl.ds(pl.multiple_of(chunk * 4 * cells, 4 * cells), 4 * cells)
+        spectral = dot(flat[here, :], table_ref[...]).reshape(4, rows, YB, NZT)
+        some = pl.ds(chunk * 4, 4)
+        out_ref[some] = (spectral + grad_ref[some].astype(F32)).astype(BF)
 
     @pl.loop(0, outer_ref.shape[1])
     def _(i):
@@ -518,7 +522,7 @@
             outer_ref[1, i, o] = s_real * b_imag - s_imag * b_real
 
 
-def last_call(rows_in, grad, weight, table, lat_inv, spec, back_spec, total):
+def last_call(rows_in, grad, table, lat_inv, spec, back_spec, total):
     channels, rows = grad.shape[:2]
     per = spec.shape[2]
     steps = NY // YB
@@ -534,7 +538,7 @@
             jax.ShapeDtypeStruct((1, channels), F32),
         ),
         in_specs=[
-            whole(rows_in), block, whole(weight), whole(table),
+            whole(rows_in), block, whole(table),
             pl.BlockSpec((1,) + lat_inv.shape[1:], lambda y: (y, 0, 0)),
             pl.BlockSpec((channels // steps,) + spec.shape[1:], lambda y: (y, 0, 0)),
             whole(back_spec), whole(total),
@@ -546,13 +550,11 @@
             pl.BlockSpec((1, channels), lambda y: (0, 0)),
         ),
         scratch_shapes=[
-            pltpu.VMEM((channels, rows, YB, NZT), F32),
             pltpu.VMEM((channels * rows * YB, 2 * LANES), BF),
-            pltpu.VMEM((channels * 8, channels * 8), BF),
         ],
         compiler_params=params(58),
         name="last",
-    )(rows_in, grad, weight, table, lat_inv, spec, back_spec, total)
+    )(rows_in, grad, table, lat_inv, spec, back_spec, total)
 
 
 def local(n, lifted_field, saturation_grad, readout, spectral_weight, point_weight, point_bias):
@@ -562,14 +564,18 @@
     stream, stream_back = stream_tables(rows * n, rows)
 
     sent = forward_call(lifted_field, narrow(forward_table), lat_whole, n)
-    rows_in, spec = mix_call(sent, spectral_weight, stream, stream_back, n)
+    rows_in, spec, point_term = mix_call(
+        sent, spectral_weight, lifted_field, stream, stream_back, point_weight, n
+    )
     grad_pre, sent_back, part = middle_call(
-        rows_in, lifted_field, saturation_grad, readout, point_bias, point_weight,
+        rows_in, lifted_field, point_term, saturation_grad, readout, point_bias,
         narrow(inverse_table.T), narrow(inverse_table), lat_inv, lat_fwd, n,
     )
-    rows_back, back_spec, total = mix_call(sent_back, spectral_weight, stream, stream_back, n, part)
+    rows_back, back_spec, point_in, total = mix_call(
+        sent_back, spectral_weight, grad_pre, stream, stream_back, point_weight, n, part
+    )
     grad_field, grad_spectral, grad_point, grad_bias = last_call(
-        rows_back, grad_pre, point_weight, narrow(forward_table.T), lat_inv, spec, back_spec, total
+        rows_back, point_in, narrow(forward_table.T), lat_inv, spec, back_spec, total
     )
     return (grad_field, grad_spectral, grad_point, grad_bias.reshape(channels))
 

time: 179 us -> 162 us (0.905)
  local copies, waits for them, and re-layouts: 9.36 us -> 0 us
  Pallas kernels: 168 us -> 160 us
    unnamed x26 -> x0, local copies, waits for them, and re-layouts: 9.36 us -> none
    pallas_call x1, Pallas kernels: 49.3 us -> 41.8 us  [middle_call(): pl.pallas_call(partial(middle_kernel, n, rr), grid=(NY // YB,), out_shape...]
    pallas_call x1, Pallas kernels: 20.1 us -> 16.1 us  [last_call(): pl.pallas_call(last_kernel, grid=(steps,), out_shape=(jax.ShapeDtypeStruc...]
    pallas_call x2, Pallas kernels: 85.9 us -> 89.9 us  [mix_call(): pl.pallas_call(partial(mix_kernel, n, rr, adjoint), out_shape=out_shape,...]
where the time goes in v2:
time: 162 us; the launch traced here: 161 us
  Pallas kernels  160 us (99%)
    pallas_call x2, Pallas kernels, mix_call(): pl.pallas_call(partial(mix_kernel, n, rr, adjoint), out_shape=out_shape,...  89.9 us
    pallas_call x1, Pallas kernels, middle_call(): pl.pallas_call(partial(middle_kernel, n, rr), grid=(NY // YB,), out_shape...  41.8 us
    pallas_call x1, Pallas kernels, last_call(): pl.pallas_call(last_kernel, grid=(steps,), out_shape=(jax.ShapeDtypeStruc...  16.1 us
    pallas_call x1, Pallas kernels, forward_call(): pl.pallas_call(partial(forward_kernel, n, rr), grid=(channels // 2,), out...  12.7 us

profile of v2, /device:TPU:0, one launch (start us, length us, event | category | flops | bytes accessed | tf_op | source)
XLA Modules:
  0.0 161.1 jit_solution(15970647734682174024)
XLA Ops:
  0.6 12.7 %forward.1.sent = bf16[16,160,72]{2,1,0:T(8,128)(2,1)} custom-call(bf16[20,4,128,512]{3,2,1,0:T(8,128)(2,1)} %field_ref.3, bf16[512,256]{1,0:T(8,128)(2,1)} %constant.23.clone.plane_ref, bf16[192,1024]{1,0:T(8,128)(2,1)} %constant.20.clone.lateral_ref), custom_call_target="tpu_custom_call" | custom-call | tf_op jit(solution)/shard_map/forward/pallas_call | solution.py:132
  13.3 39.1 %mix.1 = (bf16[10,192,256]{2,1,0:T(8,128)(2,1)}, f32[20,48,72]{2,1,0:T(8,128)}, bf16[20,4,128,512]{3,2,1,0:T(8,128)(2,1)}) custom-call(bf16[16,160,72]{2,1,0:T(8,128)(2,1)} %forward.1.sent, bf16[2,20,20,24,72]{4,3,2,1,0:T(8,128)(2,1)} %weight_hbm.3, bf16[20,4,128,512]{3,2,1,0:T(8,128)(2,1)} %field_ref.3, bf16[96,256]{1,0:T(8,128)(2,1)} %constant.21.clone.stream_ref, ...), custom_call_target="tpu_custom_call" | custom-call | tf_op jit(solution)/shard_map/mix/pallas_call | solution.py:319
  52.4 41.8 %middle.1 = (bf16[20,4,128,512]{3,2,1,0:T(8,128)(2,1)}, bf16[16,160,72]{2,1,0:T(8,128)(2,1)}, f32[24,128]{1,0:T(8,128)}) custom-call(f32[20]{0:T(128)} %readout_ref.1, f32[20]{0:T(128)} %bias_ref.1, bf16[10,192,256]{2,1,0:T(8,128)(2,1)} %get-tuple-element.18.rows_ref, bf16[20,4,128,512]{3,2,1,0:T(8,128)(2,1)} %field_ref.3, ...), custom_call_target="tpu_custom_call" | custom-call | tf_op jit(solution)/shard_map/middle/pallas_call | solution.py:462
  94.3 50.7 %adjoint_mix.1 = (bf16[10,192,256]{2,1,0:T(8,128)(2,1)}, f32[20,48,72]{2,1,0:T(8,128)}, bf16[20,4,128,512]{3,2,1,0:T(8,128)(2,1)}, f32[24,128]{1,0:T(8,128)}) custom-call(bf16[16,160,72]{2,1,0:T(8,128)(2,1)} %get-tuple-element.20.sent, bf16[2,20,20,24,72]{4,3,2,1,0:T(8,128)(2,1)} %weight_hbm.3, bf16[20,4,128,512]{3,2,1,0:T(8,128)(2,1)} %get-tuple-element.21.field_hbm, ...), custom_call_target="tpu_custom_call" | custom-call | tf_op jit(solution)/shard_map/adjoint_mix/pallas_call | solution.py:319
  145.0 16.1 %last.1 = (bf16[20,4,128,512]{3,2,1,0:T(8,128)(2,1)}, f32[2,20,20,24,72]{4,3,2,1,0:T(8,128)}, f32[20,20]{1,0:T(8,128)}, f32[1,20]{1,0:T(1,128)}) custom-call(bf16[10,192,256]{2,1,0:T(8,128)(2,1)} %get-tuple-element.23.rows_ref, bf16[20,4,128,512]{3,2,1,0:T(8,128)(2,1)} %get-tuple-element.24.grad_ref, bf16[256,512]{1,0:T(8,128)(2,1)} %constant.26.clone.table_ref, ...), custom_call_target="tpu_custom_call" | custom-call | tf_op jit(solution)/shard_map/last/pallas_call | solution.py:531

commit v3 on v2

--- a/solution.py
+++ b/solution.py
@@ -125,33 +125,28 @@
     pack(spectrum, out_ref, 0, n, rr)
 
 
-def forward_call(field, plane_table, lateral_whole, n):
-    channels, rows = field.shape[:2]
-    rr = 2 * rows
-    per = KY * KZT // n
-    return pl.pallas_call(
-        partial(forward_kernel, n, rr),
-        grid=(channels // 2,),
-        out_shape=jax.ShapeDtypeStruct((n, channels * rr, per), BF),
-        in_specs=[
-            pl.BlockSpec((2, rows, NY, NZT), lambda c: (c, 0, 0, 0)),
-            pl.BlockSpec(plane_table.shape, lambda c: (0, 0)),
-            pl.BlockSpec(lateral_whole.shape, lambda c: (0, 0)),
-        ],
-        out_specs=pl.BlockSpec((n, 2 * rr, per), lambda c: (0, c, 0)),
-        compiler_params=params(60),
-        name="forward",
-    )(field, plane_table, lateral_whole)
-
-
-def exchange(n, source, target, send, recv, local):
+def forward_part(n, rr, field_hbm, plane_ref, lateral_ref, sent, first, count):
+    rows = field_hbm.shape[1]
+    per = sent.shape[2]
+    pltpu.emit_pipeline(
+        lambda field_ref, out_ref: forward_kernel(
+            n, rr, field_ref, plane_ref, lateral_ref, out_ref
+        ),
+        grid=(count,),
+        in_specs=[pl.BlockSpec((2, rows, NY, NZT), lambda c: (c + first, 0, 0, 0))],
+        out_specs=[pl.BlockSpec((n, 2 * rr, per), lambda c: (0, c + first, 0))],
+    )(field_hbm, sent)
+
+
+def exchange(n, source, target, send, recv, local, first, count):
     me, group = lax.axis_index("gx"), lax.axis_index("groups")
+    rows = pl.ds(first, count)
     copies = []
     for k in range(1, n):
         peer = lax.rem(me + k, n)
         copy = pltpu.make_async_remote_copy(
-            src_ref=source.at[peer],
-            dst_ref=target.at[me],
+            src_ref=source.at[peer, rows],
+            dst_ref=target.at[me, rows],
             send_sem=send.at[k],
             recv_sem=recv.at[k],
             device_id=(group, peer),
@@ -159,10 +154,9 @@
         )
         copy.start()
         copies.append(copy)
-    own = pltpu.make_async_copy(source.at[me], target.at[me], local)
+    own = pltpu.make_async_copy(source.at[me, rows], target.at[me, rows], local)
     own.start()
-    own.wait()
-    return copies
+    return copies + [own]
 
 
 def spread_parts(n, source, target, send, recv, local):
@@ -181,22 +175,22 @@
         copies.append(copy)
     own = pltpu.make_async_copy(source, target.at[me], local)
     own.start()
-    own.wait()
-    return copies
-
-
-def mix_kernel(
-    n, rr, adjoint, sent, weight_hbm, field_hbm, stream_ref, back_ref, point_ref, *refs
-):
+    return copies + [own]
+
+
+def mix_kernel(n, rr, adjoint, weight_hbm, field_hbm, stream_ref, back_ref, point_ref, *refs):
     if adjoint:
-        part_ref, rows_out, spec_out, mixed_hbm, total_ref, *refs = refs
+        sent, part_ref, rows_out, spec_out, mixed_hbm, total_ref, *refs = refs
         *refs, parts, part_send, part_recv, part_local = refs
     else:
-        rows_out, spec_out, mixed_hbm, *refs = refs
+        plane_ref, lateral_ref, rows_out, spec_out, mixed_hbm, *refs = refs
+        *refs, sent = refs
     got, weights, mixed_wire, got_back, kron, send, recv, local, weight_sem = refs
     rows = field_hbm.shape[1]
     channels = spec_out.shape[0]
     per = spec_out.shape[2]
+    pairs = channels // 2
+    early = pairs // 2
     me, group = lax.axis_index("gx"), lax.axis_index("groups")
     barrier = pltpu.get_barrier_semaphore()
     for k in range(1, n):
@@ -205,15 +199,31 @@
         )
     fetch = pltpu.make_async_copy(weight_hbm, weights, weight_sem)
     fetch.start()
-    pl.semaphore_wait(barrier, n - 1)
-    copies = exchange(n, sent, got, send.at[0], recv.at[0], local.at[0])
+
+    def out(source, target, slot, first, count):
+        return exchange(
+            n, source, target, send.at[slot], recv.at[slot], local.at[slot],
+            first * 2 * rr, count * 2 * rr,
+        )
+
+    if adjoint:
+        pl.semaphore_wait(barrier, n - 1)
+        copies = out(sent, got, 0, 0, pairs)
+        shares = spread_parts(n, part_ref, parts, part_send, part_recv, part_local)
+    else:
+        forward_part(n, rr, field_hbm, plane_ref, lateral_ref, sent, 0, early)
+        pl.semaphore_wait(barrier, n - 1)
+        copies = out(sent, got, 0, 0, early)
+        forward_part(n, rr, field_hbm, plane_ref, lateral_ref, sent, early, pairs - early)
+        copies += out(sent, got, 1, early, pairs - early)
+        shares = []
     point = point_ref[...] if adjoint else point_ref[...].astype(F32).T.astype(BF)
     kron[...] = kronecker(point, channels)
     pointwise(kron, field_hbm, mixed_hbm, 0, rows // 2)
     for copy in copies:
         copy.wait()
 
-    @pl.loop(0, channels // 2)
+    @pl.loop(0, pairs)
     def _(pair):
         block = got[:, pl.ds(pl.multiple_of(pair * 2 * rr, 16), 2 * rr), :]
         both = dot(stream_ref[...], block.reshape(n * 2 * rr, per))
@@ -222,8 +232,7 @@
 
     fetch.wait()
 
-    @pl.loop(0, channels // 2)
-    def _(pair):
+    def mix(pair):
         results = []
         for half in range(2):
             o = 2 * pair + half
@@ -247,15 +256,14 @@
             n, 2 * rr, per
         )
 
-    copies = exchange(n, mixed_wire, got_back, send.at[1], recv.at[1], local.at[1])
-    if adjoint:
-        shares = spread_parts(n, part_ref, parts, part_send, part_recv, part_local)
+    pl.loop(0, early)(mix)
+    copies = out(mixed_wire, got_back, 2, 0, early)
+    pl.loop(early, pairs)(mix)
+    copies += out(mixed_wire, got_back, 3, early, pairs - early)
     pointwise(kron, field_hbm, mixed_hbm, rows // 2, rows - rows // 2)
-    for copy in copies:
+    for copy in copies + shares:
         copy.wait()
     if adjoint:
-        for copy in shares:
-            copy.wait()
         total = parts[0]
         for d in range(1, n):
             total = total + parts[d]
@@ -283,30 +291,31 @@
         rows_out[pair] = jnp.concatenate(halves, axis=1).astype(BF)
 
 
-def mix_call(sent, weight, field, stream, stream_back, point, n, part=None):
-    channels = weight.shape[1]
-    rr = sent.shape[1] // channels
-    per = sent.shape[2]
-    adjoint = part is not None
+def mix_call(weight, field, stream, stream_back, point, n, sent=None, part=None, tables=None):
+    channels, rows = field.shape[:2]
+    rr = 2 * rows
+    per = weight.shape[4]
+    adjoint = sent is not None
+    wire = (n, channels * rr, per)
     vmem = pl.BlockSpec(memory_space=pltpu.VMEM)
+    hbm = pl.BlockSpec(memory_space=pl.ANY)
     out_shape = [
         jax.ShapeDtypeStruct((channels // 2, KY * rr, 2 * LANES), BF),
         jax.ShapeDtypeStruct((channels, 2 * KX, per), F32),
         jax.ShapeDtypeStruct(field.shape, BF),
     ]
-    hbm = pl.BlockSpec(memory_space=pl.ANY)
     scratch = [
-        pltpu.VMEM(sent.shape, BF),
+        pltpu.VMEM(wire, BF),
         pltpu.VMEM(weight.shape, BF),
-        pltpu.VMEM(sent.shape, BF),
-        pltpu.VMEM(sent.shape, BF),
+        pltpu.VMEM(wire, BF),
+        pltpu.VMEM(wire, BF),
         pltpu.VMEM((channels * 8, channels * 8), BF),
-        pltpu.SemaphoreType.DMA((2, n)),
-        pltpu.SemaphoreType.DMA((2, n)),
-        pltpu.SemaphoreType.DMA((2,)),
+        pltpu.SemaphoreType.DMA((4, n)),
+        pltpu.SemaphoreType.DMA((4, n)),
+        pltpu.SemaphoreType.DMA((4,)),
         pltpu.SemaphoreType.DMA(()),
     ]
-    operands = [sent, weight, field, stream, stream_back, point]
+    operands = [weight, field, stream, stream_back, point]
     if adjoint:
         out_shape.append(jax.ShapeDtypeStruct(part.shape, F32))
         scratch += [
@@ -315,15 +324,18 @@
             pltpu.SemaphoreType.DMA((n,)),
             pltpu.SemaphoreType.DMA(()),
         ]
-        operands.append(part)
+        operands += [sent, part]
+    else:
+        scratch.append(pltpu.VMEM(wire, BF))
+        operands += list(tables)
     return pl.pallas_call(
         partial(mix_kernel, n, rr, adjoint),
         out_shape=out_shape,
-        in_specs=[vmem, hbm, hbm] + [vmem] * (len(operands) - 3),
+        in_specs=[hbm, hbm] + [vmem] * (len(operands) - 2),
         out_specs=[vmem, vmem, hbm] + [vmem] * (len(out_shape) - 3),
         scratch_shapes=scratch,
         compiler_params=params(58, collective_id=int(adjoint), has_side_effects=True),
-        name="adjoint_mix" if adjoint else "mix",
+        name="adjoint_mix" if adjoint else "forward_mix",
     )(*operands)
 
 
@@ -446,11 +458,12 @@
         )
         sums = jnp.where(mask, corr[: channels * 8], 0.0)
         inner = best(sums, spread, (((1,), (0,)), ((), ())))
+        point = best(spread, inner, (((0,), (0,)), ((), ())))
+        bias = best(corr[channels * 8 : channels * 8 + 8], spread, (((1,), (0,)), ((), ())))
         total_ref[...] = jnp.zeros_like(total_ref)
-        total_ref[:channels, :channels] = best(spread, inner, (((0,), (0,)), ((), ())))
-        total_ref[channels : channels + 4, :channels] = best(
-            corr[channels * 8 : channels * 8 + 4], spread, (((1,), (0,)), ((), ()))
-        )
+        for at in range(0, channels + 4, 4):
+            piece = point[at : at + 4] if at < channels else bias[:4]
+            total_ref[:4, at // 4 * channels : (at // 4 + 1) * channels] = piece
 
 
 def middle_call(rows_in, field, point, sat, readout, bias, inverse, back, lat_inv, lat_fwd, n):
@@ -465,7 +478,7 @@
         out_shape=(
             jax.ShapeDtypeStruct(field.shape, BF),
             jax.ShapeDtypeStruct((n, channels * rr, per), BF),
-            jax.ShapeDtypeStruct((channels + 4, LANES), F32),
+            jax.ShapeDtypeStruct((8, LANES), F32),
         ),
         in_specs=[
             scalars, scalars,
@@ -480,7 +493,7 @@
         out_specs=(
             pl.BlockSpec((channels, rows, YB, NZT), lambda y: (0, 0, y, 0)),
             pl.BlockSpec((n, channels * rr, per), lambda y: (0, 0, 0)),
-            pl.BlockSpec((channels + 4, LANES), lambda y: (0, 0)),
+            pl.BlockSpec((8, LANES), lambda y: (0, 0)),
         ),
         scratch_shapes=[
             pltpu.VMEM((channels // 2, KY * rr, 2 * LANES), F32),
@@ -501,8 +514,9 @@
 
     @pl.when(pl.program_id(0) == 0)
     def _():
-        point_ref[...] = total_ref[:channels, :channels]
-        bias_ref[...] = total_ref[channels : channels + 1, :channels]
+        for at in range(0, channels, 4):
+            point_ref[at : at + 4, :] = total_ref[:4, at // 4 * channels : (at // 4 + 1) * channels]
+        bias_ref[...] = total_ref[:1, channels // 4 * channels : (channels // 4 + 1) * channels]
 
     planes(rows_ref, lat_inv_ref[0], flat, channels, cells)
 
@@ -563,16 +577,16 @@
     lat_fwd, lat_inv, lat_whole = lateral_tables(rows)
     stream, stream_back = stream_tables(rows * n, rows)
 
-    sent = forward_call(lifted_field, narrow(forward_table), lat_whole, n)
     rows_in, spec, point_term = mix_call(
-        sent, spectral_weight, lifted_field, stream, stream_back, point_weight, n
+        spectral_weight, lifted_field, stream, stream_back, point_weight, n,
+        tables=(narrow(forward_table), lat_whole),
     )
     grad_pre, sent_back, part = middle_call(
         rows_in, lifted_field, point_term, saturation_grad, readout, point_bias,
         narrow(inverse_table.T), narrow(inverse_table), lat_inv, lat_fwd, n,
     )
     rows_back, back_spec, point_in, total = mix_call(
-        sent_back, spectral_weight, grad_pre, stream, stream_back, point_weight, n, part
+        spectral_weight, grad_pre, stream, stream_back, point_weight, n, sent=sent_back, part=part
     )
     grad_field, grad_spectral, grad_point, grad_bias = last_call(
         rows_back, point_in, narrow(forward_table.T), lat_inv, spec, back_spec, total

time: 162 us -> 149 us (0.920)
  Pallas kernels: 160 us -> 147 us
    pallas_call x1 -> x0, Pallas kernels: 12.7 us -> none  [forward_call(): pl.pallas_call(partial(forward_kernel, n, rr), grid=(channels // 2,), out...]
where the time goes in v3:
time: 149 us; the launch traced here: 148 us
  Pallas kernels  147 us (99%)
    pallas_call x2, Pallas kernels, mix_call(): pl.pallas_call(partial(mix_kernel, n, rr, adjoint), out_shape=out_shape,...  89.1 us
    pallas_call x1, Pallas kernels, middle_call(): pl.pallas_call(partial(middle_kernel, n, rr), grid=(NY // YB,), out_shape...  41.9 us
    pallas_call x1, Pallas kernels, last_call(): pl.pallas_call(last_kernel, grid=(steps,), out_shape=(jax.ShapeDtypeStruc...  16.2 us

profile of v3, /device:TPU:0, one launch (start us, length us, event | category | flops | bytes accessed | tf_op | source)
XLA Modules:
  0.0 147.8 jit_solution(12778060912063699226)
XLA Ops:
  0.6 47.9 %forward_mix.1 = (bf16[10,192,256]{2,1,0:T(8,128)(2,1)}, f32[20,48,72]{2,1,0:T(8,128)}, bf16[20,4,128,512]{3,2,1,0:T(8,128)(2,1)}) custom-call(bf16[2,20,20,24,72]{4,3,2,1,0:T(8,128)(2,1)} %weight_hbm.3, bf16[20,4,128,512]{3,2,1,0:T(8,128)(2,1)} %field_ref.1, bf16[96,256]{1,0:T(8,128)(2,1)} %constant.21.clone.stream_ref, ...), custom_call_target="tpu_custom_call" | custom-call | tf_op jit(solution)/shard_map/forward_mix/pallas_call | solution.py:331
  48.5 41.9 %middle.1 = (bf16[20,4,128,512]{3,2,1,0:T(8,128)(2,1)}, bf16[16,160,72]{2,1,0:T(8,128)(2,1)}, f32[8,128]{1,0:T(8,128)}) custom-call(f32[20]{0:T(128)} %readout_ref.1, f32[20]{0:T(128)} %bias_ref.1, bf16[10,192,256]{2,1,0:T(8,128)(2,1)} %get-tuple-element.18.rows_ref, bf16[20,4,128,512]{3,2,1,0:T(8,128)(2,1)} %field_ref.1, ...), custom_call_target="tpu_custom_call" | custom-call | tf_op jit(solution)/shard_map/middle/pallas_call | solution.py:475
  90.4 41.2 %adjoint_mix.1 = (bf16[10,192,256]{2,1,0:T(8,128)(2,1)}, f32[20,48,72]{2,1,0:T(8,128)}, bf16[20,4,128,512]{3,2,1,0:T(8,128)(2,1)}, f32[8,128]{1,0:T(8,128)}) custom-call(bf16[2,20,20,24,72]{4,3,2,1,0:T(8,128)(2,1)} %weight_hbm.3, bf16[20,4,128,512]{3,2,1,0:T(8,128)(2,1)} %get-tuple-element.20.field_hbm, bf16[96,256]{1,0:T(8,128)(2,1)} %constant.21.clone.stream_ref, ...), custom_call_target="tpu_custom_call" | custom-call | tf_op jit(solution)/shard_map/adjoint_mix/pallas_call | solution.py:331
  131.6 16.2 %last.1 = (bf16[20,4,128,512]{3,2,1,0:T(8,128)(2,1)}, f32[2,20,20,24,72]{4,3,2,1,0:T(8,128)}, f32[20,20]{1,0:T(8,128)}, f32[1,20]{1,0:T(1,128)}) custom-call(bf16[10,192,256]{2,1,0:T(8,128)(2,1)} %get-tuple-element.23.rows_ref, bf16[20,4,128,512]{3,2,1,0:T(8,128)(2,1)} %get-tuple-element.24.grad_ref, bf16[256,512]{1,0:T(8,128)(2,1)} %constant.26.clone.table_ref, ...), custom_call_target="tpu_custom_call" | custom-call | tf_op jit(solution)/shard_map/last/pallas_call | solution.py:545

commit v4 on v3

--- a/solution.py
+++ b/solution.py
@@ -401,7 +401,7 @@
 
     planes(rows_ref, lat_inv_ref[0], flat, channels, cells)
 
-    @pl.loop(0, channels // 2)
+    @pl.loop(0, channels // 2, unroll=5)
     def _(pair):
         here = pl.ds(pl.multiple_of(pair * 2 * cells, 2 * cells), 2 * cells)
         both = dot(flat[here, :], inverse_ref[...])
@@ -413,7 +413,7 @@
             grad = (readout_ref[o] * sat * gelu_slope(pre)).astype(BF)
             grad_ref[o] = grad.reshape(rows, YB, NZT)
 
-    @pl.loop(0, rows)
+    @pl.loop(0, rows, unroll=True)
     def _(x):
         lefts, rights = [], []
         for yb in range(YB // 8):
@@ -520,7 +520,7 @@
 
     planes(rows_ref, lat_inv_ref[0], flat, channels, cells)
 
-    @pl.loop(0, channels // 4)
+    @pl.loop(0, channels // 4, unroll=5)
     def _(chunk):
         here = pl.ds(pl.multiple_of(chunk * 4 * cells, 4 * cells), 4 * cells)
         spectral = dot(flat[here, :], table_ref[...]).reshape(4, rows, YB, NZT)

time: 149 us -> 141 us (0.946)
  Pallas kernels: 147 us -> 139 us
    pallas_call x1, Pallas kernels: 41.9 us -> 35 us  [middle_call(): pl.pallas_call(partial(middle_kernel, n, rr), grid=(NY // YB,), out_shape...]
    pallas_call x1, Pallas kernels: 16.2 us -> 14.7 us  [last_call(): pl.pallas_call(last_kernel, grid=(steps,), out_shape=(jax.ShapeDtypeStruc...]
where the time goes in v4:
time: 141 us; the launch traced here: 139 us
  Pallas kernels  139 us (99%)
    pallas_call x2, Pallas kernels, mix_call(): pl.pallas_call(partial(mix_kernel, n, rr, adjoint), out_shape=out_shape,...  89.1 us
    pallas_call x1, Pallas kernels, middle_call(): pl.pallas_call(partial(middle_kernel, n, rr), grid=(NY // YB,), out_shape...  35 us
    pallas_call x1, Pallas kernels, last_call(): pl.pallas_call(last_kernel, grid=(steps,), out_shape=(jax.ShapeDtypeStruc...  14.7 us

profile of v4, /device:TPU:0, one launch (start us, length us, event | category | flops | bytes accessed | tf_op | source)
XLA Modules:
  0.0 139.5 jit_solution(3800650007846327995)
XLA Ops:
  0.6 47.9 %forward_mix.1 = (bf16[10,192,256]{2,1,0:T(8,128)(2,1)}, f32[20,48,72]{2,1,0:T(8,128)}, bf16[20,4,128,512]{3,2,1,0:T(8,128)(2,1)}) custom-call(bf16[2,20,20,24,72]{4,3,2,1,0:T(8,128)(2,1)} %weight_hbm.3, bf16[20,4,128,512]{3,2,1,0:T(8,128)(2,1)} %field_ref.1, bf16[96,256]{1,0:T(8,128)(2,1)} %constant.21.clone.stream_ref, ...), custom_call_target="tpu_custom_call" | custom-call | tf_op jit(solution)/shard_map/forward_mix/pallas_call | solution.py:331
  48.5 35.0 %middle.1 = (bf16[20,4,128,512]{3,2,1,0:T(8,128)(2,1)}, bf16[16,160,72]{2,1,0:T(8,128)(2,1)}, f32[8,128]{1,0:T(8,128)}) custom-call(f32[20]{0:T(128)} %readout_ref.1, f32[20]{0:T(128)} %bias_ref.1, bf16[10,192,256]{2,1,0:T(8,128)(2,1)} %get-tuple-element.18.rows_ref, bf16[20,4,128,512]{3,2,1,0:T(8,128)(2,1)} %field_ref.1, ...), custom_call_target="tpu_custom_call" | custom-call | tf_op jit(solution)/shard_map/middle/pallas_call | solution.py:475
  83.6 41.2 %adjoint_mix.1 = (bf16[10,192,256]{2,1,0:T(8,128)(2,1)}, f32[20,48,72]{2,1,0:T(8,128)}, bf16[20,4,128,512]{3,2,1,0:T(8,128)(2,1)}, f32[8,128]{1,0:T(8,128)}) custom-call(bf16[2,20,20,24,72]{4,3,2,1,0:T(8,128)(2,1)} %weight_hbm.3, bf16[20,4,128,512]{3,2,1,0:T(8,128)(2,1)} %get-tuple-element.20.field_hbm, bf16[96,256]{1,0:T(8,128)(2,1)} %constant.21.clone.stream_ref, ...), custom_call_target="tpu_custom_call" | custom-call | tf_op jit(solution)/shard_map/adjoint_mix/pallas_call | solution.py:331
  124.8 14.7 %last.1 = (bf16[20,4,128,512]{3,2,1,0:T(8,128)(2,1)}, f32[2,20,20,24,72]{4,3,2,1,0:T(8,128)}, f32[20,20]{1,0:T(8,128)}, f32[1,20]{1,0:T(1,128)}) custom-call(bf16[10,192,256]{2,1,0:T(8,128)(2,1)} %get-tuple-element.23.rows_ref, bf16[20,4,128,512]{3,2,1,0:T(8,128)(2,1)} %get-tuple-element.24.grad_ref, bf16[256,512]{1,0:T(8,128)(2,1)} %constant.26.clone.table_ref, ...), custom_call_target="tpu_custom_call" | custom-call | tf_op jit(solution)/shard_map/last/pallas_call | solution.py:545
